TPU v7x, 128 devices: a whole 4x4x4 slice. The times are simulated.
128 devices in a mesh: gx: 4 (over x), gy: 4 (over y), gz: 8 (over z, core).
Axes of the slice: x: 4, y: 4, z: 4, core: 2. Of those that a mesh axis runs over, the one named last changes fastest.
Arguments:
- source_term: float32 [32, 128, 1024], P('gx', 'gy', 'gz'), may hold values from -8 to 8
- conductivity: float32 [32, 128, 1024], P('gx', 'gy', 'gz'), may hold values from 0.3 to 3
- jacobi_weights: float32 [3], replicated, may hold values from 0.7 to 0.95
- cotangent: float32 [32, 128, 1024], P('gx', 'gy', 'gz'), may hold values from -4 to 4
Outputs:
- solution: float32 [32, 128, 1024], P('gx', 'gy', 'gz')
- source_grad: float32 [32, 128, 1024], P('gx', 'gy', 'gz')
- weight_grad: float32 [3], replicated
All inputs are finite; a program needn't handle non-finite values.
Results may differ from a plain program's by a relative error of at most 0.0001.
Values sent between devices are 32-bit elements; how exact they have to be, the bound alone decides.
A program may use at most 128 MiB of HBM per device.

v0:
```python
import jax
import jax.numpy as jnp
from jax import lax
from jax.sharding import PartitionSpec as P

LEVELS = 3
SWEEPS = 2
COARSE_SWEEPS = 8
CYCLES = 2


def padded_2(cells, sides, width):
    for axis, dim in sides:
        count = lax.axis_size(axis)
        ends = count - 1
        head = lax.slice_in_dim(cells, 0, width, axis=dim)
        tail = lax.slice_in_dim(cells, cells.shape[dim] - width, cells.shape[dim], axis=dim)
        cells = jnp.concatenate(
            [
                lax.ppermute(tail, axis, [(i, (i + 1) % count) for i in range(ends)]),
                cells,
                lax.ppermute(head, axis, [((i + 1) % count, i) for i in range(ends)]),
            ],
            axis=dim,
        )
    return cells


def neighbours(padded):
    return [
        padded[2:, 1:-1, 1:-1],
        padded[:-2, 1:-1, 1:-1],
        padded[1:-1, 2:, 1:-1],
        padded[1:-1, :-2, 1:-1],
        padded[1:-1, 1:-1, 2:],
        padded[1:-1, 1:-1, :-2],
    ]


def coarsen(values):
    blocks = values.reshape(
        values.shape[0] // 2, 2, values.shape[1] // 2, 2, values.shape[2] // 2, 2
    )
    return jnp.sum(blocks, axis=(1, 3, 5)) * 0.125


def children_sum(values):
    blocks = values.reshape(
        values.shape[0] // 2, 2, values.shape[1] // 2, 2, values.shape[2] // 2, 2
    )
    return jnp.sum(blocks, axis=(1, 3, 5))


def refine(values):
    return jnp.repeat(jnp.repeat(jnp.repeat(values, 2, axis=0), 2, axis=1), 2, axis=2)


def build_section(coefficient, padded, factor):
    couplings = [factor * 0.5 * (coefficient + beside) for beside in neighbours(padded)]
    diagonal = (
        couplings[0] + couplings[1] + couplings[2] + couplings[3] + couplings[4] + couplings[5]
    )
    return (couplings, diagonal, 1.0 / diagonal)


def operate(current, padded, section):
    couplings, diagonal, inverse = section
    beside = neighbours(padded)
    summed = couplings[0] * beside[0]
    for direction in range(1, 6):
        summed = summed + couplings[direction] * beside[direction]
    return diagonal * current - summed


def fine_rim(values):
    return padded_2(values, (("gx", 0), ("gy", 1), ("gz", 2)), 1)


def middle_rim(values):
    return padded_2(values, (("gx", 0), ("gy", 1), ("gz", 2)), 1)


def coarse_rim(values):
    return padded_2(values, (("gx", 0), ("gy", 1), ("gz", 2)), 1)


def smooth(current, source, section, weight, rim, sweeps_count, zero_start, records):
    remaining = sweeps_count
    if zero_start:
        defect = section[2] * source
        records.append(defect)
        current = weight * defect
        remaining = sweeps_count - 1

    def sweep_step(state, unused):
        defect_now = section[2] * (source - operate(state, rim(state), section))
        return (state + weight * defect_now, defect_now)

    current, stacked = lax.scan(sweep_step, current, None, length=remaining)
    records.append(stacked)
    return current


def smooth_back(adjoint, section, weight, rim, zero_start, records):
    weight_part = jnp.zeros((), jnp.float32)
    source_part = jnp.zeros_like(adjoint)
    stacked = records.pop()

    def back_step(carry, defect):
        adjoint_now, source_now, weight_now = carry
        weight_now = weight_now + jnp.sum(adjoint_now * defect)
        pushed = weight * (section[2] * adjoint_now)
        source_now = source_now + pushed
        adjoint_now = adjoint_now - operate(pushed, rim(pushed), section)
        return ((adjoint_now, source_now, weight_now), None)

    (adjoint, source_part, weight_part), unused = lax.scan(
        back_step, (adjoint, source_part, weight_part), stacked, reverse=True
    )
    if zero_start:
        defect = records.pop()
        weight_part = weight_part + jnp.sum(adjoint * defect)
        source_part = source_part + weight * (section[2] * adjoint)
    return (adjoint, source_part, weight_part)


def coarse_forward(source, section, weight, records):
    return smooth(None, source, section, weight, coarse_rim, COARSE_SWEEPS, True, records)


def coarse_backward(adjoint, section, weight, records, partials):
    ignored, source_part, weight_part = smooth_back(
        adjoint, section, weight, coarse_rim, True, records
    )
    partials[LEVELS - 1] = partials[LEVELS - 1] + weight_part
    return (None, source_part)


def vcycle(current, source, level_index, sections, rims, weights, zero_start, records):
    section = sections[level_index]
    if level_index == LEVELS - 1:
        return coarse_forward(source, section, weights[level_index], records)
    rim = rims[level_index]
    current = smooth(
        current, source, section, weights[level_index], rim, SWEEPS, zero_start, records
    )
    defect = source - operate(current, rim(current), section)
    correction = vcycle(
        None, coarsen(defect), level_index + 1, sections, rims, weights, True, records
    )
    current = current + refine(correction)
    return smooth(current, source, section, weights[level_index], rim, SWEEPS, False, records)


def ascend(adjoint, level_index, sections, rims, weights, zero_start, records, partials):
    section = sections[level_index]
    if level_index == LEVELS - 1:
        return coarse_backward(adjoint, section, weights[level_index], records, partials)
    rim = rims[level_index]
    adjoint, source_part, weight_part = smooth_back(
        adjoint, section, weights[level_index], rim, False, records
    )
    ignored, coarse_source = ascend(
        children_sum(adjoint), level_index + 1, sections, rims, weights, True, records, partials
    )
    moved = refine(coarse_source) * 0.125
    source_part = source_part + moved
    adjoint = adjoint - operate(moved, rim(moved), section)
    adjoint, early_source, early_weight = smooth_back(
        adjoint, section, weights[level_index], rim, zero_start, records
    )
    partials[level_index] = partials[level_index] + weight_part + early_weight
    return (adjoint, source_part + early_source)


def body(source_term, conductivity, jacobi_weights, cotangent):
    sections = []
    coefficient = conductivity
    for level_index in range(LEVELS):
        factor = 0.25**level_index
        if level_index < LEVELS - 1:
            padded = padded_2(coefficient, (("gx", 0), ("gy", 1), ("gz", 2)), 1)
            sections.append(build_section(coefficient, padded, factor))
        else:
            padded = padded_2(coefficient, (("gx", 0), ("gy", 1), ("gz", 2)), 1)
            sections.append(build_section(coefficient, padded, factor))
        if level_index < LEVELS - 1:
            coefficient = coarsen(coefficient)
    rims = [fine_rim, middle_rim]
    records = []
    current = None
    for cycle_index in range(CYCLES):
        current = vcycle(
            current, source_term, 0, sections, rims, jacobi_weights, cycle_index == 0, records
        )
    partials = [jnp.zeros((), jnp.float32) for level_index in range(LEVELS + 1)]
    adjoint = cotangent
    source_grad = None
    for cycle_index in reversed(range(CYCLES)):
        adjoint, source_part = ascend(
            adjoint, 0, sections, rims, jacobi_weights, cycle_index == 0, records, partials
        )
        source_grad = source_part if source_grad is None else source_grad + source_part
    local_sums = jnp.stack(partials[:LEVELS])
    summed = lax.psum(local_sums, ("gx", "gy", "gz"))
    shared = jnp.stack(
        [jnp.zeros((), jnp.float32) for level_index in range(LEVELS - 1)] + [partials[LEVELS]]
    )
    cells = source_term.size * lax.axis_size("gx") * lax.axis_size("gy") * lax.axis_size("gz")
    weight_grad = (summed + shared) / cells
    return (current, source_grad, weight_grad)


def solution(mesh):
    return jax.shard_map(
        body,
        mesh=mesh,
        in_specs=(P("gx", "gy", "gz"), P("gx", "gy", "gz"), P(), P("gx", "gy", "gz")),
        out_specs=(P("gx", "gy", "gz"), P("gx", "gy", "gz"), P()),
        check_vma=False,
    )
```

profile of v0, /device:TPU:1, one launch (start us, length us, event | category | flops | bytes accessed | tf_op | source)
XLA Modules:
  0.0 2146.8 jit_solution(4081801806394968333)
XLA Ops:
  8.3 10.4 reshape.155
  157.0 9.7 reshape.156
  243.3 195.6 %while.250 = (s32[]{:T(128)}, f32[2,8,32]{2,1,0:T(8,128)S(1)}, f32[7,2,8,32]{3,2,1,0:T(8,128)}, f32[]{:T(128)}, f32[2,8,32]{2,1,0:T(8,128)}, /*index=5*/f32[2,8,...) while((s32[]{:T(128)}, f32[2,8,32]{2,1,0:T(8,128)S(1)}, ...), condition=%wide.region_5.6_spmd, body=%wide.region_4.5_spmd.sunk | while | flops 16386 | bytes 265561 | solution.py:99
  282.1 5.2 collective-permute-start.3
  309.6 5.2 collective-permute-start.3
  337.1 5.2 collective-permute-start.3
  364.6 5.2 collective-permute-start.3
  392.1 5.3 collective-permute-start.3
  419.7 5.4 collective-permute-start.3
  446.9 56.5 %while.251 = (s32[]{:T(128)}, f32[4,16,64]{2,1,0:T(8,128)}, f32[2,4,16,64]{3,2,1,0:T(8,128)}, f32[]{:T(128)}, f32[4,16,64]{2,1,0:T(8,128)S(1)}, /*index=5*/f32[4...) while((s32[]{:T(128)}, f32[4,16,64]{2,1,0:T(8,128)}, ...), condition=%wide.region_7.8_spmd, body=%wide.region_6.7_spmd.sunk | while | flops 124418 | bytes 843317 | solution.py:99
  511.4 56.9 %while.252 = (s32[]{:T(128)}, f32[8,32,128]{2,1,0:T(8,128)S(1)}, f32[2,8,32,128]{3,2,1,0:T(8,128)}, f32[]{:T(128)}, f32[8,32,128]{2,1,0:T(8,128)S(1)}, /*index=5...) while((s32[]{:T(128)}, f32[8,32,128]{2,1,0:T(8,128)S(1)}, ...), condition=%wide.region_9.10_spmd, body=%wide.region_8.9_spmd.sunk | while | flops 971778 | bytes 4340149 | solution.py:99
  569.0 56.8 %while.253 = (s32[]{:T(128)}, f32[8,32,128]{2,1,0:T(8,128)S(1)}, f32[2,8,32,128]{3,2,1,0:T(8,128)}, f32[]{:T(128)}, f32[8,32,128]{2,1,0:T(8,128)S(1)}, /*index=5...) while((s32[]{:T(128)}, f32[8,32,128]{2,1,0:T(8,128)S(1)}, ...), condition=%wide.region_11.12_spmd, body=%wide.region_10.11_spmd.sunk | while | flops 971778 | bytes 4340149 | solution.py:99
  642.8 15.5 collective-permute-start.131
  677.6 10.5 reshape.164
  734.7 6.0 collective-permute-start.143
  751.6 200.0 %while.254 = (s32[]{:T(128)}, f32[2,8,32]{2,1,0:T(8,128)S(1)}, f32[7,2,8,32]{3,2,1,0:T(8,128)}, f32[]{:T(128)}, f32[2,8,32]{2,1,0:T(8,128)}, /*index=5*/f32[2,8,...) while((s32[]{:T(128)}, f32[2,8,32]{2,1,0:T(8,128)S(1)}, ...), condition=%wide.region_15.16_spmd, body=%wide.region_14.15_spmd.sunk | while | flops 16386 | bytes 265561 | solution.py:99
  762.6 5.2 collective-permute-start.27
  769.6 6.3 collective-permute-start.28
  794.2 5.3 collective-permute-start.27
  821.8 5.3 collective-permute-start.27
  849.5 5.3 collective-permute-start.27
  877.1 5.3 collective-permute-start.27
  904.8 5.3 collective-permute-start.27
  932.4 5.3 collective-permute-start.27
  959.5 56.4 %while.255 = (s32[]{:T(128)}, f32[4,16,64]{2,1,0:T(8,128)}, f32[2,4,16,64]{3,2,1,0:T(8,128)}, f32[]{:T(128)}, f32[4,16,64]{2,1,0:T(8,128)S(1)}, /*index=5*/f32[4...) while((s32[]{:T(128)}, f32[4,16,64]{2,1,0:T(8,128)}, ...), condition=%wide.region_17.18_spmd, body=%wide.region_16.17_spmd.sunk | while | flops 124418 | bytes 843317 | solution.py:99
  1021.6 56.8 %while.256 = (s32[]{:T(128)}, f32[8,32,128]{2,1,0:T(8,128)S(1)}, f32[2,8,32,128]{3,2,1,0:T(8,128)}, f32[]{:T(128)}, f32[8,32,128]{2,1,0:T(8,128)S(1)}, /*index=5...) while((s32[]{:T(128)}, f32[8,32,128]{2,1,0:T(8,128)S(1)}, ...), condition=%wide.region_19.20_spmd, body=%wide.region_18.19_spmd.sunk | while | flops 971778 | bytes 4340149 | solution.py:99
  1079.1 60.5 %while.257 = (s32[]{:T(128)}, f32[8,32,128]{2,1,0:T(8,128)}, f32[8,32,128]{2,1,0:T(8,128)}, f32[]{:T(128)}, f32[]{:T(128)}, /*index=5*/f32[8,32,128]{2,1,0:T(8,1...) while((s32[]{:T(128)}, f32[8,32,128]{2,1,0:T(8,128)}, ...), condition=%wide.region_22.23_spmd.clone, body=%wide.region_20.22_spmd.clone.sunk | while | flops 1424388 | bytes 3071079 | solution.py:117
  1139.7 10.5 reshape.172
  1154.8 55.5 %while.258 = (s32[]{:T(128)}, f32[4,16,64]{2,1,0:T(8,128)}, f32[4,16,64]{2,1,0:T(8,128)}, f32[]{:T(128)}, f32[]{:T(128)}, /*index=5*/f32[4,16,64]{2,1,0:T(8,128)...) while((s32[]{:T(128)}, f32[4,16,64]{2,1,0:T(8,128)}, ...), condition=%wide.region_26.27_spmd.clone, body=%wide.region_24.26_spmd.clone.sunk | while | flops 184836 | bytes 453031 | solution.py:117
  1215.1 194.3 %while.259 = (s32[]{:T(128)}, f32[2,8,32]{2,1,0:T(8,128)}, f32[2,8,32]{2,1,0:T(8,128)}, f32[]{:T(128)}, f32[]{:T(128)}, /*index=5*/f32[2,8,32]{2,1,0:T(8,128)S(1...) while((s32[]{:T(128)}, f32[2,8,32]{2,1,0:T(8,128)}, ...), condition=%wide.region_30.31_spmd.clone, body=%wide.region_28.30_spmd.clone.sunk | while | flops 25092 | bytes 80591 | solution.py:117
  1458.7 6.0 collective-permute-start.155
  1501.5 5.9 collective-permute-start.161
  1522.2 62.2 %while.260 = (s32[]{:T(128)}, f32[8,32,128]{2,1,0:T(8,128)S(1)}, f32[8,32,128]{2,1,0:T(8,128)}, f32[]{:T(128)}, f32[]{:T(128)}, /*index=5*/f32[8,32,128]{2,1,0:T...) while((s32[]{:T(128)}, f32[8,32,128]{2,1,0:T(8,128)S(1)}, ...), condition=%wide.region_33.34_spmd.clone, body=%wide.region_31.33_spmd.clone.sunk | while | flops 1424388 | bytes 3071079 | solution.py:117
  1539.8 6.1 collective-permute-start.64
  1584.4 59.4 %while.261 = (s32[]{:T(128)}, f32[8,32,128]{2,1,0:T(8,128)S(1)}, f32[8,32,128]{2,1,0:T(8,128)}, f32[]{:T(128)}, f32[]{:T(128)}, /*index=5*/f32[8,32,128]{2,1,0:T...) while((s32[]{:T(128)}, f32[8,32,128]{2,1,0:T(8,128)S(1)}, ...), condition=%wide.region_36.37_spmd.clone, body=%wide.region_34.36_spmd.clone.sunk | while | flops 1424388 | bytes 3071079 | solution.py:117
  1643.9 9.7 reshape.174
  1658.2 53.2 %while.262 = (s32[]{:T(128)}, f32[4,16,64]{2,1,0:T(8,128)}, f32[4,16,64]{2,1,0:T(8,128)}, f32[]{:T(128)}, f32[]{:T(128)}, /*index=5*/f32[4,16,64]{2,1,0:T(8,128)...) while((s32[]{:T(128)}, f32[4,16,64]{2,1,0:T(8,128)}, ...), condition=%wide.region_40.41_spmd.clone, body=%wide.region_38.40_spmd.clone.sunk | while | flops 184836 | bytes 424275 | solution.py:117
  1716.4 195.2 %while.263 = (s32[]{:T(128)}, f32[2,8,32]{2,1,0:T(8,128)}, f32[2,8,32]{2,1,0:T(8,128)}, f32[]{:T(128)}, f32[]{:T(128)}, /*index=5*/f32[2,8,32]{2,1,0:T(8,128)S(1...) while((s32[]{:T(128)}, f32[2,8,32]{2,1,0:T(8,128)}, ...), condition=%wide.region_44.45_spmd.clone, body=%wide.region_42.44_spmd.clone.sunk | while | flops 25092 | bytes 80591 | solution.py:117
  1754.6 5.2 collective-permute-start.81
  1782.5 5.2 collective-permute-start.81
  1810.4 5.2 collective-permute-start.81
  1838.4 5.2 collective-permute-start.81
  1866.3 5.2 collective-permute-start.81
  1894.2 5.2 collective-permute-start.81
  1960.9 6.0 collective-permute-start.173
  1999.4 6.0 collective-permute-start.179
  2050.9 6.1 collective-permute-start.185
  2074.5 68.0 %psum.7 = f32[3]{0:T(128)S(1)} all-reduce(f32[3]{0:T(128)S(1)} %pad_maximum_fusion.583), channel_id=1, replica_groups=mesh['gx'=4,'gy'=4,'gz'=8] {'gx','gy','gz'}, use_global_device_ids=true, to_apply=%region_53.54 | all-reduce | flops 3 | bytes 24 | tf_op jit(solution)/shard_map/psum | solution.py:205
  (1817 shorter events, 1835.7 us)
Async XLA Ops:
  2.9 27.6 %collective-permute-start.85 = (f32[1,32,128]{2,1,0:T(8,128)S(1)}, f32[1,32,128]{2,1,0:T(8,128)S(1)}, u32[]{:S(2)}, u32[]{:S(2)}) collective-permute-start(f32[1,32,128]{2,1,0:T(8,128)S(1)} %get-tuple-element.4060), channel_id=1, source_target_pairs={{0,32},{32,64},{64,96},{1,33},{33,65},{65,97},{2,34},{34,66},{66,9... | collective-permute-start | bytes 49160 | tf_op jit(solution)/shard_map/ppermute | solution.py:20
  6.9 23.7 %collective-permute-start.84 = (f32[1,32,128]{2,1,0:T(8,128)S(1)}, f32[1,32,128]{2,1,0:T(8,128)S(1)}, u32[]{:S(2)}, u32[]{:S(2)}) collective-permute-start(f32[1,32,128]{2,1,0:T(8,128)S(1)} %get-tuple-element.4059), channel_id=1, source_target_pairs={{32,0},{64,32},{96,64},{33,1},{65,33},{97,65},{34,2},{66,34},{98,6... | collective-permute-start | bytes 49160 | tf_op jit(solution)/shard_map/ppermute | solution.py:22
  23.4 42.9 %collective-permute-start.96 = (f32[1,16,64]{2,1,0:T(8,128)}, f32[1,16,64]{2,1,0:T(8,128)S(1)}, u32[]{:S(2)}, u32[]{:S(2)}) collective-permute-start(f32[1,16,64]{2,1,0:T(8,128)} %get-tuple-element.4118), channel_id=1, source_target_pairs={{32,0},{64,32},{96,64},{33,1},{65,33},{97,65},{34,2},{66,34},{98,6... | collective-permute-start | bytes 12296 | tf_op jit(solution)/shard_map/ppermute | solution.py:22
  24.7 41.6 %collective-permute-start.97 = (f32[1,16,64]{2,1,0:T(8,128)}, f32[1,16,64]{2,1,0:T(8,128)S(1)}, u32[]{:S(2)}, u32[]{:S(2)}) collective-permute-start(f32[1,16,64]{2,1,0:T(8,128)} %get-tuple-element.4119), channel_id=1, source_target_pairs={{0,32},{32,64},{64,96},{1,33},{33,65},{65,97},{2,34},{34,66},{66,9... | collective-permute-start | bytes 12296 | tf_op jit(solution)/shard_map/ppermute | solution.py:20
  36.9 12.8 collective-permute-start.88
  61.4 13.2 collective-permute-start.91
  65.0 9.6 collective-permute-start.90
  67.0 12.7 collective-permute-start.98
  68.2 11.5 collective-permute-start.99
  84.6 8.9 collective-permute-start.94
  107.8 14.7 collective-permute-start.103
  112.7 10.8 collective-permute-start.102
  114.7 14.7 collective-permute-start.100
  116.6 13.4 collective-permute-start.101
  134.8 9.5 collective-permute-start.106
  172.1 11.5 collective-permute-start.108
  173.3 10.2 collective-permute-start.109
  178.3 10.6 collective-permute-start.114
  179.6 9.3 collective-permute-start.115
  183.6 10.6 collective-permute-start.110
  184.9 9.3 collective-permute-start.111
  188.9 13.0 collective-permute-start.116
  190.2 11.7 collective-permute-start.117
  204.7 12.1 collective-permute-start.120
  205.9 10.9 collective-permute-start.121
  210.3 11.8 collective-permute-start.118
  212.2 9.9 collective-permute-start.119
  224.0 9.9 collective-permute-start.124
  640.8 22.3 %collective-permute-start.130 = (f32[10,34,1]{2,1,0:T(8,128)}, f32[10,34,1]{2,1,0:T(8,128)}, u32[]{:S(2)}, u32[]{:S(2)}) collective-permute-start(f32[10,34,1]{2,1,0:T(8,128)} %get-tuple-element.4006), channel_id=1, source_target_pairs={{1,0},{2,1},{3,2},{4,3},{5,4},{6,5},{7,6},{9,8},{10,9},{11,10},{12... | collective-permute-start | bytes 4088 | tf_op jit(solution)/shard_map/ppermute | solution.py:22
  642.8 20.4 collective-permute-start.131
  732.8 8.3 collective-permute-start.142
  1413.5 13.1 collective-permute-start.144
  1417.5 9.1 collective-permute-start.145
  1456.5 8.3 collective-permute-start.154
  1471.0 14.8 collective-permute-start.157
  1477.6 9.1 collective-permute-start.156
  1499.6 9.8 collective-permute-start.160
  1501.5 8.7 collective-permute-start.161
  1539.8 9.1 collective-permute-start.64
  1916.4 12.4 collective-permute-start.162
  1920.4 8.4 collective-permute-start.163
  1958.7 8.3 collective-permute-start.172
  1972.1 11.1 collective-permute-start.175
  1997.5 9.9 collective-permute-start.178
  1999.4 9.0 collective-permute-start.179
  2036.3 10.9 collective-permute-start.183
  2049.0 11.5 collective-permute-start.184
  2050.9 9.6 collective-permute-start.185
  (550 other events, 5760.8 us)
where the time goes:
time: 2180 us; the launch traced here: 2150 us
  starting transfers between devices  1110 us (51%)
  waiting for transfers between devices  325 us (15%)
  other arithmetic  320 us (15%)
  local copies, waits for them, and re-layouts  295 us (14%)
  blocking collectives  68 us (3%)
    ppermute x195, starting transfers between devices, padded_2(): lax.ppermute(tail, axis, [(i, (i + 1) % count) for i in range(ends)])  811 us
    ppermute x195, starting transfers between devices, padded_2(): lax.ppermute(head, axis, [((i + 1) % count, i) for i in range(ends)])  299 us
    ppermute x195, waiting for transfers between devices, padded_2(): lax.ppermute(head, axis, [((i + 1) % count, i) for i in range(ends)])  259 us
    psum x1, blocking collectives, body(): summed = lax.psum(local_sums, ('gx', 'gy', 'gz'))  68 us
    ppermute x195, waiting for transfers between devices, padded_2(): lax.ppermute(tail, axis, [(i, (i + 1) % count) for i in range(ends)])  66.2 us
    add x24, other arithmetic, back_step(): source_now = source_now + pushed  64.4 us
    unnamed x159, local copies, waits for them, and re-layouts  64.3 us
    concatenate x117, other arithmetic, padded_2(): jnp.concatenate([lax.ppermute(tail, axis, [(i, (i + 1) % count) for i in...  53.7 us
  transfers between devices with their start and end apart: 390, of which 177 were waited for; matrix products, arithmetic and copies ran while one was open for 5% of the time, Pallas kernels for 0%

commit v1 on v0

v1 whole, which is shorter than its diff:
```python
import functools

import jax
import jax.numpy as jnp
from jax import lax
from jax.experimental import pallas as pl
from jax.experimental.pallas import tpu as pltpu
from jax.sharding import PartitionSpec as P

MESH = pl.DeviceIdType.MESH
CELLS = 32 * 128 * 1024
PLANES = (16, 4, 2)
WORK = (48, 32, 24)
ROWS = (64, 48, 40)
GROUP = (64, 32, 32)
OWN = (32, 16, 8)
FIRST = (16, 8, 12)
AROUND = [(ds, dy) for ds in (-1, 0, 1) for dy in (-1, 0, 1) if (ds, dy) != (0, 0)]


def lane_of(rows):
    return lax.broadcasted_iota(jnp.int32, (rows, 128), 1)


def row_of(rows):
    return lax.broadcasted_iota(jnp.int32, (rows, 128), 0)


def roll(values, shift):
    shift = shift % 128
    return values if shift == 0 else pltpu.roll(values, shift, 1)


def kernel(
    f_ref, c_ref, w_ref, g_ref, sol_ref, grad_ref, wg_ref,
    pk, tb, ef, ua, ub, fr, kk, dd, qq, tt, sv,
    c1, ua1, ub1, fr1, kk1, dd1, qq1, tt1, sv1,
    c2, ua2, ub2, fr2, kk2, dd2, qq2, sv2,
    inside0, inside1, inside2, mats,
    *rest,
):
    ex = [rest[6 * i : 6 * i + 6] for i in range(5)]
    rest = rest[30:]
    ga = [rest[2 * i : 2 * i + 2] for i in range(3)]
    po, ob, ra, rb, rc = rest[6:11]
    send_sem, recv_sem = rest[11:13]

    x, y, z = lax.axis_index("gx"), lax.axis_index("gy"), lax.axis_index("gz")
    odd = lax.rem(z, 2)

    def flip(value, parity):
        return value + parity * (3 - 2 * value)

    part = flip(x, odd)
    slab = 4 * z + part

    def peer(ds, dy):
        other = lax.rem(slab + ds + 32, 32)
        oz = lax.div(other, 4)
        ox = flip(lax.rem(other, 4), lax.rem(oz, 2))
        return (ox, lax.rem(y + dy + 4, 4), oz)

    x_peers = [(lax.rem(x + d, 4), y, z) for d in (1, 2, 3)]
    y_peers = [(x, lax.rem(y + d, 4), z) for d in (1, 2, 3)]
    z_peers = [(x, y, lax.rem(z + d, 8)) for d in range(1, 8)]
    peers = {o: peer(*o) for o in AROUND}

    barrier = pltpu.get_barrier_semaphore()
    greeted = x_peers + list(peers.values()) + [y_peers[1]] + z_peers
    for device in greeted:
        pl.semaphore_signal(barrier, inc=1, device_id=device, device_id_type=MESH)

    pending = []
    counter = [0]

    def remote(src, dst, device):
        slot = counter[0]
        counter[0] += 1
        copy = pltpu.make_async_remote_copy(
            src_ref=src, dst_ref=dst, send_sem=send_sem.at[slot], recv_sem=recv_sem.at[slot],
            device_id=device, device_id_type=MESH,
        )
        copy.start()
        pending.append(copy)
        return copy

    lane32 = lane_of(32)
    for field, ref in enumerate((c_ref, f_ref, g_ref)):
        for x1 in range(2):
            planes = [ref[4 * x1 + x0] for x0 in range(4)]
            for p in range(4):
                packed = roll(planes[0], -32 * p)
                for x0 in range(1, 4):
                    packed = jnp.where(lane32 // 32 == x0, roll(planes[x0], 32 * (x0 - p)), packed)
                pk[p, field, x1] = packed
    pl.semaphore_wait(barrier, len(greeted))
    copies = []
    for d in (1, 2, 3):
        other = lax.rem(x + d, 4)
        copies.append(remote(pk.at[flip(other, odd)], tb.at[x], (other, y, z)))

    for level, ref in enumerate((inside0, inside1, inside2)):
        rows, lanes = row_of(WORK[level]) - 8, lane_of(WORK[level]) % GROUP[level] - FIRST[level]
        own = OWN[level]
        good = (lanes >= -8) & (lanes < own + 8)
        good &= ((rows >= 0) | (y > 0)) & ((rows < own) | (y < 3))
        good &= ((lanes >= 0) | (slab > 0)) & ((lanes < own) | (slab < 31))
        ref[...] = good.astype(jnp.float32)
    src, dst = row_of(128), lane_of(128)
    for t in range(2):
        mats[t] = jnp.where(dst == (2 * (src // 64) + t) * 32 + (src % 64) // 2, 0.125, 0.0)
        mats[2 + t] = jnp.where(src == (2 * (dst // 64) + t) * 32 + (dst % 64) // 2, 1.0, 0.0)
    mats[4] = jnp.where((dst // 32 == src // 32) & (dst % 32 == 8 + (src % 32) // 2), 0.125, 0.0)
    mats[5] = jnp.where((dst // 32 == src // 32) & (src % 32 == 8 + (dst % 32) // 2), 1.0, 0.0)
    for ref in (c1, ua1, ub1, tt1, c2, ua2, ub2):
        ref[...] = jnp.zeros_like(ref)
    for ref in (tt, ua, ub, ef):
        edge = jnp.zeros(ref.shape[:-2] + (8, 128), jnp.float32)
        ref[..., 0:8, :] = edge
        ref[..., 56:64, :] = edge

    tb[x] = pk[part]
    for copy in copies:
        copy.wait_recv()

    group32 = lane32 // 64

    def build(field, unused):
        for h in range(2):
            for x1 in range(2):
                low, high = tb[h, field, x1], tb[2 + h, field, x1]
                for x0 in range(4):
                    plane = jnp.where(group32 == 0, roll(low, 16 - 32 * x0), roll(high, 80 - 32 * x0))
                    ef[field, 1 + 8 * h + 4 * x1 + x0, 16:48] = plane
        return unused

    lax.fori_loop(0, 3, build, 0)

    def pack(level, ref, bufs, count):
        zs, ys = bufs[:2]
        own, first, group = OWN[level], FIRST[level], GROUP[level]
        per = group // 8
        lanes = lane_of(own) % group
        lanes8 = lane_of(8) % group
        mine = (lanes8 >= first) & (lanes8 < first + own)

        def step(field, unused):
            for i in range(PLANES[level] // per):
                left = right = None
                for k in range(per):
                    plane = ref[field, 1 + i * per + k, 16 : 16 + own]
                    a, b = roll(plane, 8 * k - first), roll(plane, 8 * k - first - own + 8)
                    left = a if k == 0 else jnp.where(lanes // 8 == k, a, left)
                    right = b if k == 0 else jnp.where(lanes // 8 == k, b, right)
                zs[0, field, i] = left
                zs[1, field, i] = right
            for i in range(PLANES[level] // 2):
                for side, at in ((0, 16), (1, 8 + own)):
                    a, b = ref[field, 1 + 2 * i, at : at + 8], ref[field, 2 + 2 * i, at : at + 8]
                    ys[side, field, i] = jnp.where(mine, a, roll(b, group // 2))
            return unused

        lax.fori_loop(0, count, step, 0)

    def send(level, bufs):
        zs, ys, ls, rs, yl, yh = bufs
        own = OWN[level]
        low, high, face = pl.ds(0, 8), pl.ds(own + 8, 8), pl.ds(8, own)
        first, last = pl.ds(0, 8), pl.ds(own - 8, 8)
        return [
            remote(zs.at[1], ls.at[:, :, face], peers[1, 0]),
            remote(zs.at[0], rs.at[:, :, face], peers[-1, 0]),
            remote(ys.at[1], yl, peers[0, 1]),
            remote(ys.at[0], yh, peers[0, -1]),
            remote(zs.at[1, :, :, last], ls.at[:, :, low], peers[1, 1]),
            remote(zs.at[1, :, :, first], ls.at[:, :, high], peers[1, -1]),
            remote(zs.at[0, :, :, last], rs.at[:, :, low], peers[-1, 1]),
            remote(zs.at[0, :, :, first], rs.at[:, :, high], peers[-1, -1]),
        ]

    def ghosts(level, ref, count):
        planes, work, group = PLANES[level], WORK[level], GROUP[level]
        at = slice(8, 8 + work)
        lanes = lane_of(work)
        for field in range(count):
            before, after = ref[field, planes, at], ref[field, 1, at]
            ref[field, 0, at] = jnp.where(lanes < group, 0.0, roll(before, group))
            ref[field, planes + 1, at] = jnp.where(lanes >= 128 - group, 0.0, roll(after, -group))

    insides = (inside0, inside1, inside2)

    def unpack(level, ref, bufs, count):
        ls, rs, yl, yh = bufs[2:]
        own, first, group, work = OWN[level], FIRST[level], GROUP[level], WORK[level]
        per = group // 8
        lanes = lane_of(work) % group
        mine = (lanes >= first) & (lanes < first + own)
        before = lanes < first

        def step(field, unused):
            keep = insides[level][...]
            for i in range(PLANES[level] // per):
                left, right = ls[field, i], rs[field, i]
                for k in range(per):
                    plane = i * per + k
                    low, high = yl[field, plane // 2], yh[field, plane // 2]
                    if plane % 2:
                        low, high = roll(low, -(group // 2)), roll(high, -(group // 2))
                    middle = ref[field, 1 + plane, 16 : 16 + own]
                    base = jnp.concatenate([low, middle, high], axis=0)
                    sides = jnp.where(
                        before, roll(left, first - 8 - 8 * k), roll(right, first + own - 8 * k)
                    )
                    ref[field, 1 + plane, 8 : 8 + work] = jnp.where(mine, base, sides) * keep
            return unused

        lax.fori_loop(0, count, step, 0)

    def beside(ref, field, plane, work):
        here = ref[field, plane + 1, 8 : 8 + work]
        return here, [
            ref[field, plane + 2, 8 : 8 + work],
            ref[field, plane, 8 : 8 + work],
            ref[field, plane + 1, 9 : 9 + work],
            ref[field, plane + 1, 7 : 7 + work],
            roll(here, -1),
            roll(here, 1),
        ]

    def setup(level, cells, kref, dref, qref):
        work = WORK[level]
        factor = 0.5 * 0.25**level

        def step(plane, unused):
            here, around = beside(cells, 0, plane, work)
            couplings = [factor * (here + other) for other in around]
            diagonal = couplings[0]
            for coupling in couplings[1:]:
                diagonal = diagonal + coupling
            good = (insides[level][...] > 0.5) & (diagonal > 0.0)
            inverse = jnp.where(good, 1.0 / jnp.where(good, diagonal, 1.0), 0.0)
            for index, coupling in enumerate(couplings):
                kref[index, plane] = inverse * coupling
            dref[plane] = diagonal
            qref[plane] = inverse
            return unused

        lax.fori_loop(0, PLANES[level], step, 0)

    krefs, drefs, frefs, svs = (kk, kk1, kk2), (dd, dd1, dd2), (fr, fr1, fr2), (sv, sv1, sv2)

    def residual(level, ref, field, plane):
        here, around = beside(ref, field, plane, WORK[level])
        total = frefs[level][field, plane] - here
        for index in range(6):
            total = total + krefs[level][index, plane] * around[index]
        return here, total

    def sweep(level, old, new, save=None):
        weight = w_ref[level]

        def step(plane, unused):
            for field in range(2):
                here, r = residual(level, old, field, plane)
                new[field, plane + 1, 8 : 8 + WORK[level]] = here + weight * r
                if save is not None:
                    svs[level][save, field, plane] = r[8 : 8 + OWN[level]]
            return unused

        lax.fori_loop(0, PLANES[level], step, 0)
        ghosts(level, new, 2)

    def first_sweep(level, new):
        weight = w_ref[level]

        def step(plane, unused):
            for field in range(2):
                new[field, plane + 1, 8 : 8 + WORK[level]] = weight * frefs[level][field, plane]
            return unused

        lax.fori_loop(0, PLANES[level], step, 0)
        ghosts(level, new, 2)

    def defect(level, ref, out):
        work = WORK[level]

        def step(pair, unused):
            for field in range(2):
                total = None
                for side in range(2):
                    plane = 2 * pair + side
                    e = drefs[level][plane] * residual(level, ref, field, plane)[1]
                    total = e if total is None else total + e
                out[field, pair, 8 : 8 + work] = total
            return unused

        lax.fori_loop(0, PLANES[level] // 2, step, 0)

    def dot(a, b):
        return jnp.dot(a, b, precision=lax.Precision.HIGHEST, preferred_element_type=jnp.float32)

    def pairs(ref, field, plane, rows):
        even = ref[field, plane, pl.ds(0, rows // 2, stride=2), :]
        return even + ref[field, plane, pl.ds(1, rows // 2, stride=2), :]

    def restricted(level, ref, field):
        if level == 0:
            a = jnp.concatenate([pairs(ref, field, m, 64) for m in range(4)], axis=0)
            b = jnp.concatenate([pairs(ref, field, 4 + m, 64) for m in range(4)], axis=0)
            return (dot(a, mats[0]) + dot(b, mats[1])).reshape(4, 32, 128)
        a = jnp.concatenate([pairs(ref, field, m, 48) for m in range(2)], axis=0)
        return dot(a, mats[4]).reshape(2, 24, 128)

    def prolong(level, ref, out):
        for field in range(2):
            if level == 0:
                w = ref[field, 1:5, 8:40].reshape(128, 128)
                for t in range(2):
                    moved = dot(w, mats[2 + t]).reshape(4, 32, 128)
                    for m in range(4):
                        out[field, 4 * t + m, pl.ds(0, 32, stride=2), :] = moved[m]
                        out[field, 4 * t + m, pl.ds(1, 32, stride=2), :] = moved[m]
            else:
                w = ref[field, 1:3, 8:32].reshape(48, 128)
                moved = dot(w, mats[5]).reshape(2, 24, 128)
                for m in range(2):
                    out[field, m, pl.ds(0, 24, stride=2), :] = moved[m]
                    out[field, m, pl.ds(1, 24, stride=2), :] = moved[m]

    def product(level, a, b, fa, fb):
        own, first = OWN[level], FIRST[level]
        lanes = lane_of(own) % GROUP[level]
        mine = (lanes >= first) & (lanes < first + own)

        def step(plane, total):
            saved = svs[level]
            value = drefs[level][plane, 8 : 8 + own] * saved[a, fa, plane] * saved[b, fb, plane]
            value = jnp.where(mine, value, 0.0)
            for tile in range(own // 8):
                total = total + value[8 * tile : 8 * tile + 8]
            return total

        return lax.fori_loop(0, PLANES[level], step, jnp.zeros((8, 128), jnp.float32))

    def gather(bufs):
        own, land = bufs
        return [
            remote(own, land.at[1 - ds, :, :, pl.ds(8 - 8 * dy, 8)], peers[ds, dy])
            for ds, dy in AROUND
        ]

    lanes2 = lane_of(24) % 32

    def gathered(land, field, plane):
        sides = jnp.where(
            lanes2 < 12, roll(land[0, field, plane], -8), roll(land[2, field, plane], 8)
        )
        mine = (lanes2 >= 12) & (lanes2 < 20)
        return jnp.where(mine, land[1, field, plane], sides) * inside2[...]

    pack(0, ef, ex[0], 3)
    copies = send(0, ex[0])

    def add_planes(pair, unused):
        tt[0, pair, 16:48] = ef[0, 1 + 2 * pair, 16:48] + ef[0, 2 + 2 * pair, 16:48]
        return unused

    lax.fori_loop(0, 8, add_planes, 0)
    early = restricted(0, tt, 0)
    for pair in range(2):
        tt1[0, pair, 8:40] = early[2 * pair] + early[2 * pair + 1]
    early = restricted(1, tt1, 0)
    own2, land2 = ga[0]
    for plane in range(2):
        own2[0, plane] = early[plane, 8:16]
        land2[1, 0, plane, 8:16] = early[plane, 8:16]
    coarse_copies = gather(ga[0])

    for copy in copies:
        copy.wait_recv()
    unpack(0, ef, ex[0], 3)
    ghosts(0, ef, 1)
    setup(0, ef, kk, dd, qq)

    def right_side(plane, unused):
        for field in range(2):
            fr[field, plane] = qq[plane] * ef[1 + field, plane + 1, 8:56]
        return unused

    lax.fori_loop(0, 16, right_side, 0)

    first_sweep(0, ua)
    sweep(0, ua, ub, 0)
    defect(0, ub, tt)

    def coarse_right_side(level, source, fine):
        for field in range(2):
            values = restricted(level, fine, field)
            for plane in range(PLANES[level + 1]):
                source(field, plane, values[plane])

    def keep1(field, plane, value):
        fr1[field, plane] = value

    coarse_right_side(0, keep1, tt)

    def add_planes_whole(pair, unused):
        tt[0, pair, 8:56] = ef[0, 1 + 2 * pair, 8:56] + ef[0, 2 + 2 * pair, 8:56]
        return unused

    lax.fori_loop(0, 8, add_planes_whole, 0)
    cells = restricted(0, tt, 0)
    for plane in range(4):
        c1[0, plane + 1, 8:40] = cells[plane] * inside1[...]
    ghosts(1, c1, 1)
    setup(1, c1, kk1, dd1, qq1)
    for copy in coarse_copies:
        copy.wait_recv()
    for plane in range(2):
        c2[0, plane + 1, 8:32] = gathered(land2, 0, plane)
    ghosts(2, c2, 1)
    setup(2, c2, kk2, dd2, qq2)

    def scale1():
        for field in range(2):
            for plane in range(4):
                fr1[field, plane] = qq1[plane] * fr1[field, plane]

    def middle(cycle):
        first_sweep(1, ua1)
        sweep(1, ua1, ub1, 2 * cycle)
        defect(1, ub1, tt1)
        own, land = ga[1 + cycle]

        def keep2(field, plane, value):
            scaled = qq2[plane, 8:16] * value[8:16]
            own[field, plane] = scaled
            land[1, field, plane, 8:16] = scaled

        coarse_right_side(1, keep2, tt1)
        copies = gather(ga[1 + cycle])
        if cycle == 0:
            pack(1, ub1, ex[1], 2)
            more = send(1, ex[1])
        for copy in copies:
            copy.wait_recv()
        for field in range(2):
            for plane in range(2):
                fr2[field, plane] = gathered(land, field, plane)
        first_sweep(2, ua2)
        refs = (ua2, ub2)
        for index in range(1, 8):
            save = cycle if index == 3 + cycle else None
            sweep(2, refs[(index + 1) % 2], refs[index % 2], save)
        prolong(1, ub2, tt1)
        if cycle == 0:
            for copy in more:
                copy.wait_recv()
            unpack(1, ub1, ex[1], 2)
        for field in range(2):
            for plane in range(4):
                ub1[field, plane + 1, 8:40] = (
                    ub1[field, plane + 1, 8:40] + tt1[field, plane // 2, 8:40]
                )
        ghosts(1, ub1, 2)
        sweep(1, ub1, ua1, 1 + 2 * cycle)
        sweep(1, ua1, ub1)

    def correct(ref):
        prolong(0, ub1, tt)

        def step(plane, unused):
            for field in range(2):
                ref[field, plane + 1, 16:48] = (
                    ref[field, plane + 1, 16:48] + tt[field, lax.div(plane, 2), 16:48]
                )
            return unused

        lax.fori_loop(0, 16, step, 0)

    def fine_halo(ref, bufs):
        pack(0, ref, bufs, 2)
        for copy in send(0, bufs):
            copy.wait_recv()
        unpack(0, ref, bufs, 2)
        ghosts(0, ref, 2)

    scale1()
    middle(0)
    correct(ub)
    fine_halo(ub, ex[2])
    sweep(0, ub, ua)
    sweep(0, ua, ub, 1)
    sweep(0, ub, ua, 2)
    sweep(0, ua, ub)
    defect(0, ub, tt)

    def keep_c1(field, plane, value):
        ua1[field, plane + 1, 8:40] = value

    coarse_right_side(0, keep_c1, tt)
    pack(1, ua1, ex[3], 2)
    for copy in send(1, ex[3]):
        copy.wait_recv()
    unpack(1, ua1, ex[3], 2)
    for field in range(2):
        for plane in range(4):
            fr1[field, plane] = qq1[plane] * ua1[field, plane + 1, 8:40]
    middle(1)
    correct(ub)
    fine_halo(ub, ex[4])
    sweep(0, ub, ua, 3)

    scale = 1.0 / CELLS
    sums = [
        2.0 * (product(0, 0, 3, 0, 1) + product(0, 3, 0, 0, 1)) + 4.0 * product(0, 1, 2, 0, 1),
        16.0
        * (
            product(1, 0, 3, 0, 1)
            + product(1, 3, 0, 0, 1)
            + product(1, 1, 2, 0, 1)
            + product(1, 2, 1, 0, 1)
        ),
        512.0 * (product(2, 0, 1, 0, 1) + product(2, 1, 0, 0, 1)),
    ]
    for level in range(3):
        ra[z, 8 * level : 8 * level + 8] = sums[level] * scale
    copies_a = [remote(ra.at[z], ra.at[z], device) for device in z_peers]

    sweep(0, ua, ub)

    def leave(field, unused):
        for h in range(2):
            for x1 in range(2):
                planes = [ub[field, 1 + 8 * h + 4 * x1 + x0, 16:48] for x0 in range(4)]
                for g in range(2):
                    packed = roll(planes[0], -64 * g - 16)
                    for x0 in range(1, 4):
                        packed = jnp.where(
                            lane32 // 32 == x0, roll(planes[x0], 32 * x0 - 64 * g - 16), packed
                        )
                    po[2 * g + h, field, x1] = packed
        return unused

    lax.fori_loop(0, 2, leave, 0)
    copies_o = []
    for d in (1, 2, 3):
        other = lax.rem(x + d, 4)
        copies_o.append(remote(po.at[other], ob.at[part], (other, y, z)))
    ob[part] = po[x]

    for copy in copies_a:
        copy.wait_recv()
    total = ra[0]
    for index in range(1, 8):
        total = total + ra[index]
    rb[y] = total
    copies_b = [remote(rb.at[y], rb.at[y], device) for device in y_peers]

    for copy in copies_o:
        copy.wait_recv()
    for field, ref in enumerate((sol_ref, grad_ref)):
        for x1 in range(2):
            quarters = [ob[p, field, x1] for p in range(4)]
            for x0 in range(4):
                out = roll(quarters[0], -32 * x0)
                for p in range(1, 4):
                    out = jnp.where(lane32 // 32 == p, roll(quarters[p], 32 * (p - x0)), out)
                ref[4 * x1 + x0] = out

    for copy in copies_b:
        copy.wait_recv()
    total = rb[0]
    for index in range(1, 4):
        total = total + rb[index]
    rc[x] = total
    copies_c = [remote(rc.at[x], rc.at[x], device) for device in x_peers]
    for copy in copies_c:
        copy.wait_recv()
    total = rc[0]
    for index in range(1, 4):
        total = total + rc[index]
    for level in range(3):
        wg_ref[level] = jnp.sum(total[8 * level : 8 * level + 8])
    for copy in pending:
        copy.wait_send()


def f32(*shape):
    return pltpu.VMEM(shape, jnp.float32)


def exchange_buffers(level, count):
    own, strips, half = OWN[level], PLANES[level] * 8 // GROUP[level], PLANES[level] // 2
    return [
        f32(2, count, strips, own, 128),
        f32(2, count, half, 8, 128),
        f32(count, strips, own + 16, 128),
        f32(count, strips, own + 16, 128),
        f32(count, half, 8, 128),
        f32(count, half, 8, 128),
    ]


def level_buffers(level):
    planes, work, rows, own = PLANES[level], WORK[level], ROWS[level], OWN[level]
    out = [
        f32(2, planes + 2, rows, 128),
        f32(2, planes + 2, rows, 128),
        f32(2, planes, work, 128),
        f32(6, planes, work, 128),
        f32(planes, work, 128),
        f32(planes, work, 128),
    ]
    if level < 2:
        out.append(f32(2, planes // 2, rows, 128))
    out.append(f32(4 if level < 2 else 2, 2, planes, own, 128))
    return out


def body(source_term, conductivity, jacobi_weights, cotangent):
    scratch = [f32(4, 3, 2, 32, 128), f32(4, 3, 2, 32, 128), f32(3, 18, 64, 128)]
    scratch += level_buffers(0)
    scratch += [f32(1, 6, 48, 128)] + level_buffers(1)
    scratch += [f32(1, 4, 40, 128)] + level_buffers(2)
    scratch += [f32(WORK[level], 128) for level in range(3)] + [f32(6, 128, 128)]
    for level, count in ((0, 3), (1, 2), (0, 2), (1, 2), (0, 2)):
        scratch += exchange_buffers(level, count)
    for count in (1, 2, 2):
        scratch += [f32(count, 2, 8, 128), f32(3, count, 2, 24, 128)]
    scratch += [f32(4, 2, 2, 32, 128), f32(4, 2, 2, 32, 128)]
    scratch += [f32(8, 24, 128), f32(4, 24, 128), f32(4, 24, 128)]
    copies = 3 + 8 * 8 + 3 + 13
    scratch += [pltpu.SemaphoreType.DMA((copies,)), pltpu.SemaphoreType.DMA((copies,))]
    vmem = pl.BlockSpec(memory_space=pltpu.VMEM)
    smem = pl.BlockSpec(memory_space=pltpu.SMEM)
    block = jax.ShapeDtypeStruct(source_term.shape, jnp.float32)
    return pl.pallas_call(
        kernel,
        out_shape=(block, block, jax.ShapeDtypeStruct((3,), jnp.float32)),
        in_specs=[vmem, vmem, smem, vmem],
        out_specs=(vmem, vmem, smem),
        scratch_shapes=scratch,
        compiler_params=pltpu.CompilerParams(
            collective_id=0, has_side_effects=True, vmem_limit_bytes=48 * 2**20
        ),
    )(source_term, conductivity, jacobi_weights, cotangent)


def solution(mesh):
    return jax.shard_map(
        body,
        mesh=mesh,
        in_specs=(P("gx", "gy", "gz"), P("gx", "gy", "gz"), P(), P("gx", "gy", "gz")),
        out_specs=(P("gx", "gy", "gz"), P("gx", "gy", "gz"), P()),
        check_vma=False,
    )
```

time: 2180 us -> 92.3 us (0.04); the launches traced: 2150 us -> 90.9 us
  starting transfers between devices: 1110 us -> 0 us
  waiting for transfers between devices: 325 us -> 0 us
  other arithmetic: 320 us -> 0 us
  local copies, waits for them, and re-layouts: 295 us -> 5.18 us
  Pallas kernels: 0 us -> 85.1 us
  blocking collectives: 68 us -> 0 us
    ppermute x390 -> x0, starting transfers between devices: 1110 us -> none  [the longest x195 811 us: padded_2(): lax.ppermute(tail, axis, [(i, (i + 1) % count) for i in range(ends)])]
    ppermute x390 -> x0, waiting for transfers between devices: 325 us -> none  [the longest x195 259 us: padded_2(): lax.ppermute(head, axis, [((i + 1) % count, i) for i in range(ends)])]
    add x59 -> x0, other arithmetic: 110 us -> none  [the longest x24 64.4 us: back_step(): source_now = source_now + pushed]
    pallas_call x0 -> x1, Pallas kernels: none -> 85.1 us  [body(): pl.pallas_call(kernel, out_shape=(block, block, jax.ShapeDtypeStruct((3,)...]
    reshape x15 -> x0, local copies, waits for them, and re-layouts: 71 us -> none  [the longest x5 36.3 us: coarsen(): values.reshape(values.shape[0] // 2, 2, values.shape[1] // 2, 2, values.s...]
    psum x1 -> x0, blocking collectives: 68 us -> none  [body(): summed = lax.psum(local_sums, ('gx', 'gy', 'gz'))]
    slice x169 -> x0, local copies, waits for them, and re-layouts: 65.4 us -> none  [the longest x98 49.2 us: padded_2(): head = lax.slice_in_dim(cells, 0, width, axis=dim)]
    unnamed x159 -> x11, local copies, waits for them, and re-layouts: 64.3 us -> 5.18 us
  transfers between devices with their start and end apart: 390 -> 0, of which waited for: 177 -> 0; matrix products, arithmetic and copies ran while one was open for 5% -> 0% of each run, Pallas kernels for 0% -> 0%
where the time goes in v1:
time: 92.3 us; the launch traced here: 90.9 us
  Pallas kernels  85.1 us (92%)
  local copies, waits for them, and re-layouts  5.18 us (6%)
    pallas_call x1, Pallas kernels, body(): pl.pallas_call(kernel, out_shape=(block, block, jax.ShapeDtypeStruct((3,)...  85.1 us
    unnamed x11, local copies, waits for them, and re-layouts  5.18 us

profile of v1, /device:TPU:1, one launch (start us, length us, event | category | flops | bytes accessed | tf_op | source)
XLA Modules:
  0.0 90.9 jit_solution(9689694424549108167)
XLA Ops:
  0.6 0.0 copy-start
  0.6 0.9 copy-done
  1.5 0.0 copy-start.1
  1.5 0.9 copy-done.1
  2.4 0.0 copy-start.2
  2.4 0.9 copy-done.2
  3.3 0.0 copy-start.3
  3.3 0.7 copy-done.3
  4.0 85.1 %shard_map.67 = (f32[8,32,128]{2,1,0:T(8,128)S(1)}, f32[8,32,128]{2,1,0:T(8,128)S(1)}, f32[3]{0:T(128)S(1)}) custom-call(f32[8,32,128]{2,1,0:T(8,128)S(1)} %copy-done, f32[8,32,128]{2,1,0:T(8,128)S(1)} %copy-done.1, f32[3]{0:T(128)S(1)} %copy-done.3, f32[8,32,128]{2,1,0:T(8,128)S(1)} %copy-done.2), custom_call_target="tpu_custom_call" | custom-call | tf_op jit(solution)/shard_map/pallas_call | solution.py:638
  89.1 0.7 copy.10
  89.7 0.7 copy.11
  90.4 0.5 copy.12
Async XLA Ops:
  0.6 0.9 copy-start
  1.5 0.9 copy-start.1
  2.4 0.9 copy-start.2
  3.3 0.7 copy-start.3

commit v2 on v1

--- a/solution.py
+++ b/solution.py
@@ -32,8 +32,8 @@
 
 
 def kernel(
-    f_ref, c_ref, w_ref, g_ref, sol_ref, grad_ref, wg_ref,
-    pk, tb, ef, ua, ub, fr, kk, dd, qq, tt, sv,
+    f_hbm, c_hbm, w_hbm, g_hbm, sol_ref, grad_ref, wg_ref,
+    f_ref, c_ref, g_ref, w_ref, load_sem, pkc, pkf, tbc, tbf, ef, ua, ub, fr, kk, dd, qq, tt, sv,
     c1, ua1, ub1, fr1, kk1, dd1, qq1, tt1, sv1,
     c2, ua2, ub2, fr2, kk2, dd2, qq2, sv2,
     inside0, inside1, inside2, mats,
@@ -65,6 +65,14 @@
     z_peers = [(x, y, lax.rem(z + d, 8)) for d in range(1, 8)]
     peers = {o: peer(*o) for o in AROUND}
 
+    loads = [
+        pltpu.make_async_copy(src, dst, load_sem.at[index])
+        for index, (src, dst) in enumerate(
+            ((c_hbm, c_ref), (f_hbm, f_ref), (g_hbm, g_ref), (w_hbm, w_ref))
+        )
+    ]
+    for load in loads:
+        load.start()
     barrier = pltpu.get_barrier_semaphore()
     greeted = x_peers + list(peers.values()) + [y_peers[1]] + z_peers
     for device in greeted:
@@ -85,19 +93,33 @@
         return copy
 
     lane32 = lane_of(32)
-    for field, ref in enumerate((c_ref, f_ref, g_ref)):
+
+    def quarters(ref, out, field):
         for x1 in range(2):
             planes = [ref[4 * x1 + x0] for x0 in range(4)]
             for p in range(4):
                 packed = roll(planes[0], -32 * p)
                 for x0 in range(1, 4):
                     packed = jnp.where(lane32 // 32 == x0, roll(planes[x0], 32 * (x0 - p)), packed)
-                pk[p, field, x1] = packed
+                out[p, field, x1] = packed
+
+    def scatter(out, land):
+        copies = []
+        for d in (1, 2, 3):
+            other = lax.rem(x + d, 4)
+            copies.append(remote(out.at[flip(other, odd)], land.at[x], (other, y, z)))
+        return copies
+
+    loads[0].wait()
+    quarters(c_ref, pkc, 0)
     pl.semaphore_wait(barrier, len(greeted))
-    copies = []
-    for d in (1, 2, 3):
-        other = lax.rem(x + d, 4)
-        copies.append(remote(pk.at[flip(other, odd)], tb.at[x], (other, y, z)))
+    copies_c = scatter(pkc, tbc)
+    loads[1].wait()
+    quarters(f_ref, pkf, 0)
+    loads[2].wait()
+    quarters(g_ref, pkf, 1)
+    copies_f = scatter(pkf, tbf)
+    loads[3].wait()
 
     for level, ref in enumerate((inside0, inside1, inside2)):
         rows, lanes = row_of(WORK[level]) - 8, lane_of(WORK[level]) % GROUP[level] - FIRST[level]
@@ -119,24 +141,17 @@
         ref[..., 0:8, :] = edge
         ref[..., 56:64, :] = edge
 
-    tb[x] = pk[part]
-    for copy in copies:
-        copy.wait_recv()
-
     group32 = lane32 // 64
 
-    def build(field, unused):
+    def build(land, field, to):
         for h in range(2):
             for x1 in range(2):
-                low, high = tb[h, field, x1], tb[2 + h, field, x1]
+                low, high = land[h, field, x1], land[2 + h, field, x1]
                 for x0 in range(4):
                     plane = jnp.where(group32 == 0, roll(low, 16 - 32 * x0), roll(high, 80 - 32 * x0))
-                    ef[field, 1 + 8 * h + 4 * x1 + x0, 16:48] = plane
-        return unused
-
-    lax.fori_loop(0, 3, build, 0)
-
-    def pack(level, ref, bufs, count):
+                    ef[to, 1 + 8 * h + 4 * x1 + x0, 16:48] = plane
+
+    def pack(level, ref, bufs, count, nine=False, start=0):
         zs, ys = bufs[:2]
         own, first, group = OWN[level], FIRST[level], GROUP[level]
         per = group // 8
@@ -145,19 +160,32 @@
         mine = (lanes8 >= first) & (lanes8 < first + own)
 
         def step(field, unused):
+            at = start + field
+            ninths = []
             for i in range(PLANES[level] // per):
-                left = right = None
+                left = right = left9 = right9 = None
                 for k in range(per):
-                    plane = ref[field, 1 + i * per + k, 16 : 16 + own]
+                    plane = ref[at, 1 + i * per + k, 16 : 16 + own]
                     a, b = roll(plane, 8 * k - first), roll(plane, 8 * k - first - own + 8)
                     left = a if k == 0 else jnp.where(lanes // 8 == k, a, left)
                     right = b if k == 0 else jnp.where(lanes // 8 == k, b, right)
+                    if nine:
+                        left9 = a if k == 0 else jnp.where(lanes // 8 == (k + 1) % per, a, left9)
+                        right9 = b if k == 0 else jnp.where(lanes // 8 == (k - 1) % per, b, right9)
                 zs[0, field, i] = left
                 zs[1, field, i] = right
+                ninths.append((left9, right9))
+            if nine:
+                zs[0, field, 2] = jnp.where(lanes % 8 < 4, ninths[0][0], roll(ninths[1][0], 4))
+                zs[1, field, 2] = jnp.where(lanes % 8 >= 4, ninths[0][1], roll(ninths[1][1], -4))
             for i in range(PLANES[level] // 2):
-                for side, at in ((0, 16), (1, 8 + own)):
-                    a, b = ref[field, 1 + 2 * i, at : at + 8], ref[field, 2 + 2 * i, at : at + 8]
+                for side, row in ((0, 16), (1, 8 + own)):
+                    a, b = ref[at, 1 + 2 * i, row : row + 8], ref[at, 2 + 2 * i, row : row + 8]
                     ys[side, field, i] = jnp.where(mine, a, roll(b, group // 2))
+                if nine:
+                    for side, row in ((0, 24), (1, 39)):
+                        a, b = ref[at, 1 + 2 * i, row : row + 1], ref[at, 2 + 2 * i, row : row + 1]
+                        ys[side, field, 8, i : i + 1] = jnp.where(mine[:1], a, roll(b, group // 2))
             return unused
 
         lax.fori_loop(0, count, step, 0)
@@ -167,15 +195,16 @@
         own = OWN[level]
         low, high, face = pl.ds(0, 8), pl.ds(own + 8, 8), pl.ds(8, own)
         first, last = pl.ds(0, 8), pl.ds(own - 8, 8)
+        strips = pl.ds(0, PLANES[level] * 8 // GROUP[level])
         return [
             remote(zs.at[1], ls.at[:, :, face], peers[1, 0]),
             remote(zs.at[0], rs.at[:, :, face], peers[-1, 0]),
             remote(ys.at[1], yl, peers[0, 1]),
             remote(ys.at[0], yh, peers[0, -1]),
-            remote(zs.at[1, :, :, last], ls.at[:, :, low], peers[1, 1]),
-            remote(zs.at[1, :, :, first], ls.at[:, :, high], peers[1, -1]),
-            remote(zs.at[0, :, :, last], rs.at[:, :, low], peers[-1, 1]),
-            remote(zs.at[0, :, :, first], rs.at[:, :, high], peers[-1, -1]),
+            remote(zs.at[1, :, strips, last], ls.at[:, strips, low], peers[1, 1]),
+            remote(zs.at[1, :, strips, first], ls.at[:, strips, high], peers[1, -1]),
+            remote(zs.at[0, :, strips, last], rs.at[:, strips, low], peers[-1, 1]),
+            remote(zs.at[0, :, strips, first], rs.at[:, strips, high], peers[-1, -1]),
         ]
 
     def ghosts(level, ref, count):
@@ -188,16 +217,20 @@
             ref[field, planes + 1, at] = jnp.where(lanes >= 128 - group, 0.0, roll(after, -group))
 
     insides = (inside0, inside1, inside2)
-
-    def unpack(level, ref, bufs, count):
+    has_left, has_right = (slab > 0).astype(jnp.float32), (slab < 31).astype(jnp.float32)
+    has_low, has_high = (y > 0).astype(jnp.float32), (y < 3).astype(jnp.float32)
+
+    def unpack(level, ref, bufs, count, nine=False, start=0):
         ls, rs, yl, yh = bufs[2:]
         own, first, group, work = OWN[level], FIRST[level], GROUP[level], WORK[level]
         per = group // 8
         lanes = lane_of(work) % group
         mine = (lanes >= first) & (lanes < first + own)
         before = lanes < first
+        lanes9 = lane_of(own) % group
 
         def step(field, unused):
+            at = start + field
             keep = insides[level][...]
             for i in range(PLANES[level] // per):
                 left, right = ls[field, i], rs[field, i]
@@ -206,12 +239,24 @@
                     low, high = yl[field, plane // 2], yh[field, plane // 2]
                     if plane % 2:
                         low, high = roll(low, -(group // 2)), roll(high, -(group // 2))
-                    middle = ref[field, 1 + plane, 16 : 16 + own]
+                    middle = ref[at, 1 + plane, 16 : 16 + own]
                     base = jnp.concatenate([low, middle, high], axis=0)
                     sides = jnp.where(
                         before, roll(left, first - 8 - 8 * k), roll(right, first + own - 8 * k)
                     )
-                    ref[field, 1 + plane, 8 : 8 + work] = jnp.where(mine, base, sides) * keep
+                    ref[at, 1 + plane, 8 : 8 + work] = jnp.where(mine, base, sides) * keep
+                    if nine:
+                        left9 = roll(ls[field, 2, 8 : 8 + own], 8 + 4 * i - 8 * k) * has_left
+                        right9 = roll(rs[field, 2, 8 : 8 + own], 48 - 4 * i - 8 * k) * has_right
+                        middle = ref[at, 1 + plane, 16 : 16 + own]
+                        middle = jnp.where(lanes9 == 7, left9, middle)
+                        middle = jnp.where(lanes9 == 56, right9, middle)
+                        ref[at, 1 + plane, 16 : 16 + own] = middle
+                        for rows, row, has in ((yl, 7, has_low), (yh, 56, has_high)):
+                            ninth = rows[field, 8, plane // 2 : plane // 2 + 1]
+                            if plane % 2:
+                                ninth = roll(ninth, -(group // 2))
+                            ref[at, 1 + plane, row : row + 1] = jnp.where(mine[:1], ninth * has, 0.0)
             return unused
 
         lax.fori_loop(0, count, step, 0)
@@ -245,7 +290,7 @@
             qref[plane] = inverse
             return unused
 
-        lax.fori_loop(0, PLANES[level], step, 0)
+        lax.fori_loop(0, PLANES[level], step, 0, unroll=True)
 
     krefs, drefs, frefs, svs = (kk, kk1, kk2), (dd, dd1, dd2), (fr, fr1, fr2), (sv, sv1, sv2)
 
@@ -267,7 +312,7 @@
                     svs[level][save, field, plane] = r[8 : 8 + OWN[level]]
             return unused
 
-        lax.fori_loop(0, PLANES[level], step, 0)
+        lax.fori_loop(0, PLANES[level], step, 0, unroll=True)
         ghosts(level, new, 2)
 
     def first_sweep(level, new):
@@ -278,10 +323,10 @@
                 new[field, plane + 1, 8 : 8 + WORK[level]] = weight * frefs[level][field, plane]
             return unused
 
-        lax.fori_loop(0, PLANES[level], step, 0)
+        lax.fori_loop(0, PLANES[level], step, 0, unroll=True)
         ghosts(level, new, 2)
 
-    def defect(level, ref, out):
+    def defect(level, ref, out, save=None):
         work = WORK[level]
 
         def step(pair, unused):
@@ -289,12 +334,15 @@
                 total = None
                 for side in range(2):
                     plane = 2 * pair + side
-                    e = drefs[level][plane] * residual(level, ref, field, plane)[1]
+                    r = residual(level, ref, field, plane)[1]
+                    if save is not None:
+                        svs[level][save, field, plane] = r[8 : 8 + OWN[level]]
+                    e = drefs[level][plane] * r
                     total = e if total is None else total + e
                 out[field, pair, 8 : 8 + work] = total
             return unused
 
-        lax.fori_loop(0, PLANES[level] // 2, step, 0)
+        lax.fori_loop(0, PLANES[level] // 2, step, 0, unroll=True)
 
     def dot(a, b):
         return jnp.dot(a, b, precision=lax.Precision.HIGHEST, preferred_element_type=jnp.float32)
@@ -358,8 +406,19 @@
         mine = (lanes2 >= 12) & (lanes2 < 20)
         return jnp.where(mine, land[1, field, plane], sides) * inside2[...]
 
-    pack(0, ef, ex[0], 3)
-    copies = send(0, ex[0])
+    tbc[x] = pkc[part]
+    for copy in copies_c:
+        copy.wait_recv()
+    build(tbc, 0, 0)
+    pack(0, ef, ex[0], 1, True)
+    copies_c = send(0, ex[0])
+    tbf[x] = pkf[part]
+    for copy in copies_f:
+        copy.wait_recv()
+    for field in range(2):
+        build(tbf, field, 1 + field)
+    pack(0, ef, ex[1], 2, start=1)
+    copies_f = send(0, ex[1])
 
     def add_planes(pair, unused):
         tt[0, pair, 16:48] = ef[0, 1 + 2 * pair, 16:48] + ef[0, 2 + 2 * pair, 16:48]
@@ -376,33 +435,11 @@
         land2[1, 0, plane, 8:16] = early[plane, 8:16]
     coarse_copies = gather(ga[0])
 
-    for copy in copies:
-        copy.wait_recv()
-    unpack(0, ef, ex[0], 3)
+    for copy in copies_c:
+        copy.wait_recv()
+    unpack(0, ef, ex[0], 1, True)
     ghosts(0, ef, 1)
     setup(0, ef, kk, dd, qq)
-
-    def right_side(plane, unused):
-        for field in range(2):
-            fr[field, plane] = qq[plane] * ef[1 + field, plane + 1, 8:56]
-        return unused
-
-    lax.fori_loop(0, 16, right_side, 0)
-
-    first_sweep(0, ua)
-    sweep(0, ua, ub, 0)
-    defect(0, ub, tt)
-
-    def coarse_right_side(level, source, fine):
-        for field in range(2):
-            values = restricted(level, fine, field)
-            for plane in range(PLANES[level + 1]):
-                source(field, plane, values[plane])
-
-    def keep1(field, plane, value):
-        fr1[field, plane] = value
-
-    coarse_right_side(0, keep1, tt)
 
     def add_planes_whole(pair, unused):
         tt[0, pair, 8:56] = ef[0, 1 + 2 * pair, 8:56] + ef[0, 2 + 2 * pair, 8:56]
@@ -421,6 +458,32 @@
     ghosts(2, c2, 1)
     setup(2, c2, kk2, dd2, qq2)
 
+    for copy in copies_f:
+        copy.wait_recv()
+    unpack(0, ef, ex[1], 2, start=1)
+
+    def right_side(plane, unused):
+        for field in range(2):
+            fr[field, plane] = qq[plane] * ef[1 + field, plane + 1, 8:56]
+        return unused
+
+    lax.fori_loop(0, 16, right_side, 0)
+
+    first_sweep(0, ua)
+    sweep(0, ua, ub, 0)
+    defect(0, ub, tt, 3)
+
+    def coarse_right_side(level, source, fine):
+        for field in range(2):
+            values = restricted(level, fine, field)
+            for plane in range(PLANES[level + 1]):
+                source(field, plane, values[plane])
+
+    def keep1(field, plane, value):
+        fr1[field, plane] = value
+
+    coarse_right_side(0, keep1, tt)
+
     def scale1():
         for field in range(2):
             for plane in range(4):
@@ -439,9 +502,9 @@
 
         coarse_right_side(1, keep2, tt1)
         copies = gather(ga[1 + cycle])
-        if cycle == 0:
-            pack(1, ub1, ex[1], 2)
-            more = send(1, ex[1])
+        if cycle == 1:
+            pack(1, ub1, ex[2], 2)
+            more = send(1, ex[2])
         for copy in copies:
             copy.wait_recv()
         for field in range(2):
@@ -453,10 +516,10 @@
             save = cycle if index == 3 + cycle else None
             sweep(2, refs[(index + 1) % 2], refs[index % 2], save)
         prolong(1, ub2, tt1)
-        if cycle == 0:
+        if cycle == 1:
             for copy in more:
                 copy.wait_recv()
-            unpack(1, ub1, ex[1], 2)
+            unpack(1, ub1, ex[2], 2)
         for field in range(2):
             for plane in range(4):
                 ub1[field, plane + 1, 8:40] = (
@@ -476,44 +539,44 @@
                 )
             return unused
 
-        lax.fori_loop(0, 16, step, 0)
-
-    def fine_halo(ref, bufs):
-        pack(0, ref, bufs, 2)
-        for copy in send(0, bufs):
-            copy.wait_recv()
-        unpack(0, ref, bufs, 2)
-        ghosts(0, ref, 2)
+        lax.fori_loop(0, 16, step, 0, unroll=4)
 
     scale1()
     middle(0)
     correct(ub)
-    fine_halo(ub, ex[2])
+    pack(0, ub, ex[3], 2, True)
+    for copy in send(0, ex[3]):
+        copy.wait_recv()
+    unpack(0, ub, ex[3], 2, True)
+    ghosts(0, ub, 2)
     sweep(0, ub, ua)
     sweep(0, ua, ub, 1)
     sweep(0, ub, ua, 2)
     sweep(0, ua, ub)
-    defect(0, ub, tt)
-
-    def keep_c1(field, plane, value):
-        ua1[field, plane + 1, 8:40] = value
-
-    coarse_right_side(0, keep_c1, tt)
-    pack(1, ua1, ex[3], 2)
-    for copy in send(1, ex[3]):
-        copy.wait_recv()
-    unpack(1, ua1, ex[3], 2)
-    for field in range(2):
-        for plane in range(4):
-            fr1[field, plane] = qq1[plane] * ua1[field, plane + 1, 8:40]
+    defect(0, ub, tt, 4)
+    coarse_right_side(0, keep1, tt)
+    scale1()
     middle(1)
     correct(ub)
-    fine_halo(ub, ex[4])
-    sweep(0, ub, ua, 3)
-
+    pack(0, ub, ex[4], 2)
+    copies = send(0, ex[4])
+
+    own_lanes = (lane32 % 64 >= 16) & (lane32 % 64 < 48)
+
+    def corrected(plane, total):
+        value = None
+        for field in range(2):
+            change = sv[0, 1 - field, plane] - sv[3, 1 - field, plane]
+            term = change * tt[field, lax.div(plane, 2), 16:48]
+            value = term if value is None else value + term
+        value = jnp.where(own_lanes, value * dd[plane, 8:40], 0.0)
+        return total + ((value[0:8] + value[8:16]) + (value[16:24] + value[24:32]))
+
+    moved = lax.fori_loop(0, 16, corrected, jnp.zeros((8, 128), jnp.float32), unroll=4)
     scale = 1.0 / CELLS
     sums = [
-        2.0 * (product(0, 0, 3, 0, 1) + product(0, 3, 0, 0, 1)) + 4.0 * product(0, 1, 2, 0, 1),
+        2.0 * (product(0, 0, 4, 0, 1) + product(0, 4, 0, 0, 1) - moved * (1.0 / w_ref[0]))
+        + 4.0 * product(0, 1, 2, 0, 1),
         16.0
         * (
             product(1, 0, 3, 0, 1)
@@ -527,6 +590,18 @@
         ra[z, 8 * level : 8 * level + 8] = sums[level] * scale
     copies_a = [remote(ra.at[z], ra.at[z], device) for device in z_peers]
 
+    for copy in copies:
+        copy.wait_recv()
+    unpack(0, ub, ex[4], 2)
+    ghosts(0, ub, 2)
+    sweep(0, ub, ua)
+    for copy in copies_a:
+        copy.wait_recv()
+    total = ra[0]
+    for index in range(1, 8):
+        total = total + ra[index]
+    rb[y] = total
+    copies_b = [remote(rb.at[y], rb.at[y], device) for device in y_peers]
     sweep(0, ua, ub)
 
     def leave(field, unused):
@@ -549,25 +624,6 @@
         copies_o.append(remote(po.at[other], ob.at[part], (other, y, z)))
     ob[part] = po[x]
 
-    for copy in copies_a:
-        copy.wait_recv()
-    total = ra[0]
-    for index in range(1, 8):
-        total = total + ra[index]
-    rb[y] = total
-    copies_b = [remote(rb.at[y], rb.at[y], device) for device in y_peers]
-
-    for copy in copies_o:
-        copy.wait_recv()
-    for field, ref in enumerate((sol_ref, grad_ref)):
-        for x1 in range(2):
-            quarters = [ob[p, field, x1] for p in range(4)]
-            for x0 in range(4):
-                out = roll(quarters[0], -32 * x0)
-                for p in range(1, 4):
-                    out = jnp.where(lane32 // 32 == p, roll(quarters[p], 32 * (p - x0)), out)
-                ref[4 * x1 + x0] = out
-
     for copy in copies_b:
         copy.wait_recv()
     total = rb[0]
@@ -575,6 +631,18 @@
         total = total + rb[index]
     rc[x] = total
     copies_c = [remote(rc.at[x], rc.at[x], device) for device in x_peers]
+
+    for copy in copies_o:
+        copy.wait_recv()
+    for field, ref in enumerate((sol_ref, grad_ref)):
+        for x1 in range(2):
+            parts = [ob[p, field, x1] for p in range(4)]
+            for x0 in range(4):
+                out = roll(parts[0], -32 * x0)
+                for p in range(1, 4):
+                    out = jnp.where(lane32 // 32 == p, roll(parts[p], 32 * (p - x0)), out)
+                ref[4 * x1 + x0] = out
+
     for copy in copies_c:
         copy.wait_recv()
     total = rc[0]
@@ -590,8 +658,8 @@
     return pltpu.VMEM(shape, jnp.float32)
 
 
-def exchange_buffers(level, count):
-    own, strips, half = OWN[level], PLANES[level] * 8 // GROUP[level], PLANES[level] // 2
+def exchange_buffers(level, count, nine):
+    own, strips, half = OWN[level], PLANES[level] * 8 // GROUP[level] + nine, PLANES[level] // 2 + nine
     return [
         f32(2, count, strips, own, 128),
         f32(2, count, half, 8, 128),
@@ -614,31 +682,34 @@
     ]
     if level < 2:
         out.append(f32(2, planes // 2, rows, 128))
-    out.append(f32(4 if level < 2 else 2, 2, planes, own, 128))
+    out.append(f32((5, 4, 2)[level], 2, planes, own, 128))
     return out
 
 
 def body(source_term, conductivity, jacobi_weights, cotangent):
-    scratch = [f32(4, 3, 2, 32, 128), f32(4, 3, 2, 32, 128), f32(3, 18, 64, 128)]
+    block = source_term.shape
+    scratch = [f32(*block), f32(*block), f32(*block), pltpu.SMEM((3,), jnp.float32)]
+    scratch += [pltpu.SemaphoreType.DMA((4,))]
+    scratch += [f32(4, count, 2, 32, 128) for count in (1, 2, 1, 2)] + [f32(3, 18, 64, 128)]
     scratch += level_buffers(0)
     scratch += [f32(1, 6, 48, 128)] + level_buffers(1)
     scratch += [f32(1, 4, 40, 128)] + level_buffers(2)
     scratch += [f32(WORK[level], 128) for level in range(3)] + [f32(6, 128, 128)]
-    for level, count in ((0, 3), (1, 2), (0, 2), (1, 2), (0, 2)):
-        scratch += exchange_buffers(level, count)
+    for level, count, nine in ((0, 1, 1), (0, 2, 0), (1, 2, 0), (0, 2, 1), (0, 2, 0)):
+        scratch += exchange_buffers(level, count, nine)
     for count in (1, 2, 2):
         scratch += [f32(count, 2, 8, 128), f32(3, count, 2, 24, 128)]
     scratch += [f32(4, 2, 2, 32, 128), f32(4, 2, 2, 32, 128)]
     scratch += [f32(8, 24, 128), f32(4, 24, 128), f32(4, 24, 128)]
-    copies = 3 + 8 * 8 + 3 + 13
+    copies = 6 + 8 * 8 + 3 + 13
     scratch += [pltpu.SemaphoreType.DMA((copies,)), pltpu.SemaphoreType.DMA((copies,))]
     vmem = pl.BlockSpec(memory_space=pltpu.VMEM)
     smem = pl.BlockSpec(memory_space=pltpu.SMEM)
-    block = jax.ShapeDtypeStruct(source_term.shape, jnp.float32)
+    block = jax.ShapeDtypeStruct(block, jnp.float32)
     return pl.pallas_call(
         kernel,
         out_shape=(block, block, jax.ShapeDtypeStruct((3,), jnp.float32)),
-        in_specs=[vmem, vmem, smem, vmem],
+        in_specs=[pl.BlockSpec(memory_space=pl.ANY)] * 4,
         out_specs=(vmem, vmem, smem),
         scratch_shapes=scratch,
         compiler_params=pltpu.CompilerParams(

time: 92.3 us -> 66.5 us (0.72); the launches traced: 90.9 us -> 66.4 us
  Pallas kernels: 85.1 us -> 60.5 us
    pallas_call x1, Pallas kernels: 85.1 us -> 60.5 us  [body(): pl.pallas_call(kernel, out_shape=(block, block, jax.ShapeDtypeStruct((3,)...]
where the time goes in v2:
time: 66.5 us; the launch traced here: 66.4 us
  Pallas kernels  60.5 us (91%)
  local copies, waits for them, and re-layouts  5.18 us (8%)
    pallas_call x1, Pallas kernels, body(): pl.pallas_call(kernel, out_shape=(block, block, jax.ShapeDtypeStruct((3,)...  60.5 us
    unnamed x11, local copies, waits for them, and re-layouts  5.18 us

profile of v2, /device:TPU:1, one launch (start us, length us, event | category | flops | bytes accessed | tf_op | source)
XLA Modules:
  0.0 66.4 jit_solution(11837620602421034846)
XLA Ops:
  0.6 0.0 copy-start
  0.6 0.9 %copy-done = f32[8,32,128]{2,1,0:T(8,128)S(1)} copy-done((f32[8,32,128]{2,1,0:T(8,128)S(1)}, f32[8,32,128]{2,1,0:T(8,128)}, u32[]{:S(2)}) %copy-start) | copy-done | bytes 131096
  1.5 0.0 copy-start.1
  1.5 0.9 %copy-done.1 = f32[8,32,128]{2,1,0:T(8,128)S(1)} copy-done((f32[8,32,128]{2,1,0:T(8,128)S(1)}, f32[8,32,128]{2,1,0:T(8,128)}, u32[]{:S(2)}) %copy-start.1) | copy-done | bytes 131096
  2.4 0.0 copy-start.2
  2.4 0.9 %copy-done.2 = f32[8,32,128]{2,1,0:T(8,128)S(1)} copy-done((f32[8,32,128]{2,1,0:T(8,128)S(1)}, f32[8,32,128]{2,1,0:T(8,128)}, u32[]{:S(2)}) %copy-start.2) | copy-done | bytes 131096
  3.3 0.0 copy-start.3
  3.3 0.7 copy-done.3
  4.0 60.5 %shard_map.67 = (f32[8,32,128]{2,1,0:T(8,128)S(1)}, f32[8,32,128]{2,1,0:T(8,128)S(1)}, f32[3]{0:T(128)S(1)}) custom-call(f32[8,32,128]{2,1,0:T(8,128)S(1)} %copy-done, f32[8,32,128]{2,1,0:T(8,128)S(1)} %copy-done.1, f32[3]{0:T(128)S(1)} %copy-done.3, f32[8,32,128]{2,1,0:T(8,128)S(1)} %copy-done.2), custom_call_target="tpu_custom_call" | custom-call | tf_op jit(solution)/shard_map/pallas_call | solution.py:709
  64.5 0.7 copy.10
  65.2 0.7 copy.11
  65.8 0.5 copy.12
Async XLA Ops:
  0.6 0.9 %copy-start = (f32[8,32,128]{2,1,0:T(8,128)S(1)}, f32[8,32,128]{2,1,0:T(8,128)}, u32[]{:S(2)}) copy-start(f32[8,32,128]{2,1,0:T(8,128)} %f_hbm.1) | copy-start | bytes 393220
  1.5 0.9 %copy-start.1 = (f32[8,32,128]{2,1,0:T(8,128)S(1)}, f32[8,32,128]{2,1,0:T(8,128)}, u32[]{:S(2)}) copy-start(f32[8,32,128]{2,1,0:T(8,128)} %c_hbm.1) | copy-start | bytes 393220
  2.4 0.9 %copy-start.2 = (f32[8,32,128]{2,1,0:T(8,128)S(1)}, f32[8,32,128]{2,1,0:T(8,128)}, u32[]{:S(2)}) copy-start(f32[8,32,128]{2,1,0:T(8,128)} %g_hbm.1) | copy-start | bytes 393220
  3.3 0.7 copy-start.3

commit v3 on v2

--- a/solution.py
+++ b/solution.py
@@ -78,19 +78,21 @@
     for device in greeted:
         pl.semaphore_signal(barrier, inc=1, device_id=device, device_id_type=MESH)
 
-    pending = []
-    counter = [0]
-
-    def remote(src, dst, device):
-        slot = counter[0]
-        counter[0] += 1
+    def remote(src, dst, device, slot):
         copy = pltpu.make_async_remote_copy(
             src_ref=src, dst_ref=dst, send_sem=send_sem.at[slot], recv_sem=recv_sem.at[slot],
             device_id=device, device_id_type=MESH,
         )
         copy.start()
-        pending.append(copy)
         return copy
+
+    def arrive(copies):
+        for copy in copies:
+            copy.wait_recv()
+
+    def leave_behind(copies):
+        for copy in copies:
+            copy.wait_send()
 
     lane32 = lane_of(32)
 
@@ -103,22 +105,22 @@
                     packed = jnp.where(lane32 // 32 == x0, roll(planes[x0], 32 * (x0 - p)), packed)
                 out[p, field, x1] = packed
 
-    def scatter(out, land):
+    def scatter(out, land, slot):
         copies = []
         for d in (1, 2, 3):
             other = lax.rem(x + d, 4)
-            copies.append(remote(out.at[flip(other, odd)], land.at[x], (other, y, z)))
+            copies.append(remote(out.at[flip(other, odd)], land.at[x], (other, y, z), slot + d))
         return copies
 
     loads[0].wait()
     quarters(c_ref, pkc, 0)
     pl.semaphore_wait(barrier, len(greeted))
-    copies_c = scatter(pkc, tbc)
+    way_c = scatter(pkc, tbc, 31)
     loads[1].wait()
     quarters(f_ref, pkf, 0)
     loads[2].wait()
     quarters(g_ref, pkf, 1)
-    copies_f = scatter(pkf, tbf)
+    way_f = scatter(pkf, tbf, 34)
     loads[3].wait()
 
     for level, ref in enumerate((inside0, inside1, inside2)):
@@ -190,21 +192,21 @@
 
         lax.fori_loop(0, count, step, 0)
 
-    def send(level, bufs):
+    def send(level, bufs, slot):
         zs, ys, ls, rs, yl, yh = bufs
         own = OWN[level]
         low, high, face = pl.ds(0, 8), pl.ds(own + 8, 8), pl.ds(8, own)
         first, last = pl.ds(0, 8), pl.ds(own - 8, 8)
         strips = pl.ds(0, PLANES[level] * 8 // GROUP[level])
         return [
-            remote(zs.at[1], ls.at[:, :, face], peers[1, 0]),
-            remote(zs.at[0], rs.at[:, :, face], peers[-1, 0]),
-            remote(ys.at[1], yl, peers[0, 1]),
-            remote(ys.at[0], yh, peers[0, -1]),
-            remote(zs.at[1, :, strips, last], ls.at[:, strips, low], peers[1, 1]),
-            remote(zs.at[1, :, strips, first], ls.at[:, strips, high], peers[1, -1]),
-            remote(zs.at[0, :, strips, last], rs.at[:, strips, low], peers[-1, 1]),
-            remote(zs.at[0, :, strips, first], rs.at[:, strips, high], peers[-1, -1]),
+            remote(zs.at[1], ls.at[:, :, face], peers[1, 0], slot + 0),
+            remote(zs.at[0], rs.at[:, :, face], peers[-1, 0], slot + 1),
+            remote(ys.at[1], yl, peers[0, 1], slot + 2),
+            remote(ys.at[0], yh, peers[0, -1], slot + 3),
+            remote(zs.at[1, :, strips, last], ls.at[:, strips, low], peers[1, 1], slot + 4),
+            remote(zs.at[1, :, strips, first], ls.at[:, strips, high], peers[1, -1], slot + 5),
+            remote(zs.at[0, :, strips, last], rs.at[:, strips, low], peers[-1, 1], slot + 6),
+            remote(zs.at[0, :, strips, first], rs.at[:, strips, high], peers[-1, -1], slot + 7),
         ]
 
     def ghosts(level, ref, count):
@@ -301,11 +303,11 @@
             total = total + krefs[level][index, plane] * around[index]
         return here, total
 
-    def sweep(level, old, new, save=None):
+    def sweep(level, old, new, save=None, fields=(0, 1)):
         weight = w_ref[level]
 
         def step(plane, unused):
-            for field in range(2):
+            for field in fields:
                 here, r = residual(level, old, field, plane)
                 new[field, plane + 1, 8 : 8 + WORK[level]] = here + weight * r
                 if save is not None:
@@ -313,7 +315,8 @@
             return unused
 
         lax.fori_loop(0, PLANES[level], step, 0, unroll=True)
-        ghosts(level, new, 2)
+        if len(fields) == 2:
+            ghosts(level, new, 2)
 
     def first_sweep(level, new):
         weight = w_ref[level]
@@ -345,7 +348,14 @@
         lax.fori_loop(0, PLANES[level] // 2, step, 0, unroll=True)
 
     def dot(a, b):
-        return jnp.dot(a, b, precision=lax.Precision.HIGHEST, preferred_element_type=jnp.float32)
+        high = a.astype(jnp.bfloat16)
+        rest = a - high.astype(jnp.float32)
+        mid = rest.astype(jnp.bfloat16)
+        low = (rest - mid.astype(jnp.float32)).astype(jnp.bfloat16)
+        b = b.astype(jnp.bfloat16)
+        out = jnp.dot(low, b, preferred_element_type=jnp.float32)
+        out = out + jnp.dot(mid, b, preferred_element_type=jnp.float32)
+        return out + jnp.dot(high, b, preferred_element_type=jnp.float32)
 
     def pairs(ref, field, plane, rows):
         even = ref[field, plane, pl.ds(0, rows // 2, stride=2), :]
@@ -390,11 +400,11 @@
 
         return lax.fori_loop(0, PLANES[level], step, jnp.zeros((8, 128), jnp.float32))
 
-    def gather(bufs):
+    def gather(bufs, slot):
         own, land = bufs
         return [
-            remote(own, land.at[1 - ds, :, :, pl.ds(8 - 8 * dy, 8)], peers[ds, dy])
-            for ds, dy in AROUND
+            remote(own, land.at[1 - ds, :, :, pl.ds(8 - 8 * dy, 8)], peers[ds, dy], slot + index)
+            for index, (ds, dy) in enumerate(AROUND)
         ]
 
     lanes2 = lane_of(24) % 32
@@ -407,18 +417,18 @@
         return jnp.where(mine, land[1, field, plane], sides) * inside2[...]
 
     tbc[x] = pkc[part]
-    for copy in copies_c:
-        copy.wait_recv()
+    arrive(way_c)
     build(tbc, 0, 0)
     pack(0, ef, ex[0], 1, True)
-    copies_c = send(0, ex[0])
+    halo_c = send(0, ex[0], 0)
+    leave_behind(way_c)
     tbf[x] = pkf[part]
-    for copy in copies_f:
-        copy.wait_recv()
+    arrive(way_f)
     for field in range(2):
         build(tbf, field, 1 + field)
     pack(0, ef, ex[1], 2, start=1)
-    copies_f = send(0, ex[1])
+    halo_f = send(0, ex[1], 8)
+    leave_behind(way_f)
 
     def add_planes(pair, unused):
         tt[0, pair, 16:48] = ef[0, 1 + 2 * pair, 16:48] + ef[0, 2 + 2 * pair, 16:48]
@@ -433,10 +443,10 @@
     for plane in range(2):
         own2[0, plane] = early[plane, 8:16]
         land2[1, 0, plane, 8:16] = early[plane, 8:16]
-    coarse_copies = gather(ga[0])
-
-    for copy in copies_c:
-        copy.wait_recv()
+    coarse_copies = gather(ga[0], 16)
+    leave_behind(halo_c)
+
+    arrive(halo_c)
     unpack(0, ef, ex[0], 1, True)
     ghosts(0, ef, 1)
     setup(0, ef, kk, dd, qq)
@@ -451,15 +461,14 @@
         c1[0, plane + 1, 8:40] = cells[plane] * inside1[...]
     ghosts(1, c1, 1)
     setup(1, c1, kk1, dd1, qq1)
-    for copy in coarse_copies:
-        copy.wait_recv()
+    arrive(coarse_copies)
     for plane in range(2):
         c2[0, plane + 1, 8:32] = gathered(land2, 0, plane)
     ghosts(2, c2, 1)
     setup(2, c2, kk2, dd2, qq2)
 
-    for copy in copies_f:
-        copy.wait_recv()
+    leave_behind(coarse_copies + halo_f)
+    arrive(halo_f)
     unpack(0, ef, ex[1], 2, start=1)
 
     def right_side(plane, unused):
@@ -489,7 +498,7 @@
             for plane in range(4):
                 fr1[field, plane] = qq1[plane] * fr1[field, plane]
 
-    def middle(cycle):
+    def middle(cycle, before):
         first_sweep(1, ua1)
         sweep(1, ua1, ub1, 2 * cycle)
         defect(1, ub1, tt1)
@@ -501,12 +510,12 @@
             land[1, field, plane, 8:16] = scaled
 
         coarse_right_side(1, keep2, tt1)
-        copies = gather(ga[1 + cycle])
+        copies = gather(ga[1 + cycle], (24, 8)[cycle])
         if cycle == 1:
             pack(1, ub1, ex[2], 2)
-            more = send(1, ex[2])
-        for copy in copies:
-            copy.wait_recv()
+            more = send(1, ex[2], 16)
+        leave_behind(before)
+        arrive(copies)
         for field in range(2):
             for plane in range(2):
                 fr2[field, plane] = gathered(land, field, plane)
@@ -517,8 +526,7 @@
             sweep(2, refs[(index + 1) % 2], refs[index % 2], save)
         prolong(1, ub2, tt1)
         if cycle == 1:
-            for copy in more:
-                copy.wait_recv()
+            arrive(more)
             unpack(1, ub1, ex[2], 2)
         for field in range(2):
             for plane in range(4):
@@ -528,6 +536,7 @@
         ghosts(1, ub1, 2)
         sweep(1, ub1, ua1, 1 + 2 * cycle)
         sweep(1, ua1, ub1)
+        return copies + more if cycle == 1 else copies
 
     def correct(ref):
         prolong(0, ub1, tt)
@@ -542,11 +551,12 @@
         lax.fori_loop(0, 16, step, 0, unroll=4)
 
     scale1()
-    middle(0)
+    sent = middle(0, [])
     correct(ub)
     pack(0, ub, ex[3], 2, True)
-    for copy in send(0, ex[3]):
-        copy.wait_recv()
+    fine = send(0, ex[3], 0)
+    leave_behind(sent)
+    arrive(fine)
     unpack(0, ub, ex[3], 2, True)
     ghosts(0, ub, 2)
     sweep(0, ub, ua)
@@ -556,10 +566,10 @@
     defect(0, ub, tt, 4)
     coarse_right_side(0, keep1, tt)
     scale1()
-    middle(1)
+    sent = middle(1, fine)
     correct(ub)
     pack(0, ub, ex[4], 2)
-    copies = send(0, ex[4])
+    copies = send(0, ex[4], 24)
 
     own_lanes = (lane32 % 64 >= 16) & (lane32 % 64 < 48)
 
@@ -588,23 +598,23 @@
     ]
     for level in range(3):
         ra[z, 8 * level : 8 * level + 8] = sums[level] * scale
-    copies_a = [remote(ra.at[z], ra.at[z], device) for device in z_peers]
-
-    for copy in copies:
-        copy.wait_recv()
+    copies_a = [remote(ra.at[z], ra.at[z], device, 38 + i) for i, device in enumerate(z_peers)]
+    leave_behind(sent)
+
+    arrive(copies)
     unpack(0, ub, ex[4], 2)
     ghosts(0, ub, 2)
     sweep(0, ub, ua)
-    for copy in copies_a:
-        copy.wait_recv()
+    arrive(copies_a)
     total = ra[0]
     for index in range(1, 8):
         total = total + ra[index]
     rb[y] = total
-    copies_b = [remote(rb.at[y], rb.at[y], device) for device in y_peers]
-    sweep(0, ua, ub)
-
-    def leave(field, unused):
+    copies_b = [remote(rb.at[y], rb.at[y], device, 45 + i) for i, device in enumerate(y_peers)]
+    leave_behind(copies + copies_a)
+    copies_o = []
+    for field in range(2):
+        sweep(0, ua, ub, None, (field,))
         for h in range(2):
             for x1 in range(2):
                 planes = [ub[field, 1 + 8 * h + 4 * x1 + x0, 16:48] for x0 in range(4)]
@@ -614,44 +624,41 @@
                         packed = jnp.where(
                             lane32 // 32 == x0, roll(planes[x0], 32 * x0 - 64 * g - 16), packed
                         )
-                    po[2 * g + h, field, x1] = packed
-        return unused
-
-    lax.fori_loop(0, 2, leave, 0)
-    copies_o = []
-    for d in (1, 2, 3):
-        other = lax.rem(x + d, 4)
-        copies_o.append(remote(po.at[other], ob.at[part], (other, y, z)))
-    ob[part] = po[x]
-
-    for copy in copies_b:
-        copy.wait_recv()
+                    po[field, 2 * g + h, x1] = packed
+        sent = []
+        for d in (1, 2, 3):
+            other = lax.rem(x + d, 4)
+            sent.append(
+                remote(po.at[field, other], ob.at[field, part], (other, y, z), 50 + 3 * field + d)
+            )
+        copies_o.append(sent)
+        ob[field, part] = po[field, x]
+
+    arrive(copies_b)
     total = rb[0]
     for index in range(1, 4):
         total = total + rb[index]
     rc[x] = total
-    copies_c = [remote(rc.at[x], rc.at[x], device) for device in x_peers]
-
-    for copy in copies_o:
-        copy.wait_recv()
+    copies_c = [remote(rc.at[x], rc.at[x], device, 48 + i) for i, device in enumerate(x_peers)]
+    leave_behind(copies_b)
+
     for field, ref in enumerate((sol_ref, grad_ref)):
+        arrive(copies_o[field])
         for x1 in range(2):
-            parts = [ob[p, field, x1] for p in range(4)]
+            parts = [ob[field, p, x1] for p in range(4)]
             for x0 in range(4):
                 out = roll(parts[0], -32 * x0)
                 for p in range(1, 4):
                     out = jnp.where(lane32 // 32 == p, roll(parts[p], 32 * (p - x0)), out)
                 ref[4 * x1 + x0] = out
 
-    for copy in copies_c:
-        copy.wait_recv()
+    arrive(copies_c)
     total = rc[0]
     for index in range(1, 4):
         total = total + rc[index]
     for level in range(3):
         wg_ref[level] = jnp.sum(total[8 * level : 8 * level + 8])
-    for copy in pending:
-        copy.wait_send()
+    leave_behind(copies_c + copies_o[0] + copies_o[1])
 
 
 def f32(*shape):
@@ -699,9 +706,9 @@
         scratch += exchange_buffers(level, count, nine)
     for count in (1, 2, 2):
         scratch += [f32(count, 2, 8, 128), f32(3, count, 2, 24, 128)]
-    scratch += [f32(4, 2, 2, 32, 128), f32(4, 2, 2, 32, 128)]
+    scratch += [f32(2, 4, 2, 32, 128), f32(2, 4, 2, 32, 128)]
     scratch += [f32(8, 24, 128), f32(4, 24, 128), f32(4, 24, 128)]
-    copies = 6 + 8 * 8 + 3 + 13
+    copies = 57
     scratch += [pltpu.SemaphoreType.DMA((copies,)), pltpu.SemaphoreType.DMA((copies,))]
     vmem = pl.BlockSpec(memory_space=pltpu.VMEM)
     smem = pl.BlockSpec(memory_space=pltpu.SMEM)
@@ -709,11 +716,11 @@
     return pl.pallas_call(
         kernel,
         out_shape=(block, block, jax.ShapeDtypeStruct((3,), jnp.float32)),
-        in_specs=[pl.BlockSpec(memory_space=pl.ANY)] * 4,
+        in_specs=[pl.BlockSpec(memory_space=pltpu.HBM)] * 4,
         out_specs=(vmem, vmem, smem),
         scratch_shapes=scratch,
         compiler_params=pltpu.CompilerParams(
-            collective_id=0, has_side_effects=True, vmem_limit_bytes=48 * 2**20
+            collective_id=0, has_side_effects=True, vmem_limit_bytes=62 * 2**20
         ),
     )(source_term, conductivity, jacobi_weights, cotangent)
 

time: 66.5 us -> 62.4 us (0.938)
  local copies, waits for them, and re-layouts: 5.18 us -> 2.79 us
  Pallas kernels: 60.5 us -> 58.3 us
    unnamed x11 -> x7, local copies, waits for them, and re-layouts: 5.18 us -> 2.79 us
    pallas_call x1, Pallas kernels: 60.5 us -> 58.3 us  [body(): pl.pallas_call(kernel, out_shape=(block, block, jax.ShapeDtypeStruct((3,)...]
where the time goes in v3:
time: 62.4 us; the launch traced here: 61.7 us
  Pallas kernels  58.3 us (93%)
  local copies, waits for them, and re-layouts  2.79 us (4%)
  between operations  0.65 us (1%)
    pallas_call x1, Pallas kernels, body(): pl.pallas_call(kernel, out_shape=(block, block, jax.ShapeDtypeStruct((3,)...  58.3 us
    unnamed x7, local copies, waits for them, and re-layouts  2.79 us

profile of v3, /device:TPU:1, one launch (start us, length us, event | category | flops | bytes accessed | tf_op | source)
XLA Modules:
  0.0 61.7 jit_solution(11998939424569998345)
XLA Ops:
  0.6 58.3 %shard_map.67 = (f32[8,32,128]{2,1,0:T(8,128)}, f32[8,32,128]{2,1,0:T(8,128)}, f32[3]{0:T(128)}) custom-call(f32[8,32,128]{2,1,0:T(8,128)} %f_hbm.1, f32[8,32,128]{2,1,0:T(8,128)} %c_hbm.1, f32[3]{0:T(128)} %w_hbm.1, f32[8,32,128]{2,1,0:T(8,128)} %g_hbm.1), custom_call_target="tpu_custom_call" | custom-call | tf_op jit(solution)/shard_map/pallas_call | solution.py:716
  58.9 0.0 copy-start
  58.9 1.6 %copy.10 = f32[8,32,128]{2,1,0:T(8,128)} copy(f32[8,32,128]{2,1,0:T(8,128)} %get-tuple-element.6) | data formatting | bytes 262144
  60.6 0.0 copy-done
  60.6 0.0 copy-start.1
  60.6 0.7 %copy.11 = f32[8,32,128]{2,1,0:T(8,128)} copy(f32[8,32,128]{2,1,0:T(8,128)S(1)} %copy-done) | data formatting | bytes 262144
  61.2 0.0 copy-done.1
  61.2 0.5 copy.12
Async XLA Ops:
  58.9 1.6 %copy-start = (f32[8,32,128]{2,1,0:T(8,128)S(1)}, f32[8,32,128]{2,1,0:T(8,128)}, u32[]{:S(2)}) copy-start(f32[8,32,128]{2,1,0:T(8,128)} %get-tuple-element.7) | copy-start | bytes 393220
  60.6 0.7 %copy-start.1 = (f32[3]{0:T(128)S(1)}, f32[3]{0:T(128)}, u32[]{:S(2)}) copy-start(f32[3]{0:T(128)} %get-tuple-element.8) | copy-start | bytes 40
